TPU v7x, 32 devices: a whole 2x2x4 slice. The times are simulated.
32 devices in a mesh: row: 4 (over z), col: 8 (over y, x, core).
Axes of the slice: x: 2, y: 2, z: 4, core: 2. Of those that a mesh axis runs over, the one named last changes fastest.
Arguments:
- features: bfloat16 [4096, 256], P(('col', 'row')), may hold values from -6 to 6
- weight: bfloat16 [256, 256], replicated, may hold values from -0.375 to 0.375
- bias: float32 [256], replicated, may hold values from -3 to 3
- grad_out: bfloat16 [4096, 256], P(('row', 'col')), may hold values from -6 to 6
- tile_rows: int32 [4, 8, 128], P('row', 'col'), may hold values from 0 to 7
- tile_cols: int32 [4, 8, 128], P('row', 'col'), may hold values from 0 to 3
- tile_counts: int32 [4, 8], P('row', 'col'), may hold values from 1 to 128, as said below
- tile_values: bfloat16 [4, 8, 128, 128, 128], P('row', 'col'), may hold values from 0 to 0.011962891
Outputs:
- output: bfloat16 [4096, 256], P(('row', 'col'))
- grad_features: bfloat16 [4096, 256], P(('col', 'row'))
- grad_weight: float32 [256, 256], replicated
- grad_bias: float32 [256], replicated
Inputs may be any that keep to these rules, and one draw needn't show every extreme that they name: `tile_counts`: some grid cell has all 128 slots live. Tile coordinates may repeat within a cell; repeated tiles add.
All inputs are finite; a program needn't handle non-finite values.
Results may differ from a plain program's by a relative error of at most 0.018.
Values may be sent and summed in bfloat16 or wider, within the bound.
A program may use at most 64 MiB of HBM per device.

v0:
```python
import jax
import jax.numpy as jnp
from jax import lax
from jax.sharding import PartitionSpec as P

GROUP = 8


def elu_value(pre):
    return jnp.where(pre > 0, pre, jnp.expm1(jnp.minimum(pre, 0.0)))


def elu_slope(pre):
    return jnp.where(pre > 0, jnp.float32(1.0), jnp.exp(jnp.minimum(pre, 0.0)))


def accumulate(values, dest_idx, src_idx, live, source, dest_tiles, transpose):
    side = values.shape[-1]
    width = source.shape[-1]
    group_size = GROUP
    blocks_all = source.reshape(source.shape[0] // side, side, width)

    def one_group(step, acc):
        first = step * group_size
        part_values = lax.dynamic_slice_in_dim(values, first, group_size, 0)
        part_dest = lax.dynamic_slice_in_dim(dest_idx, first, group_size, 0)
        part_src = lax.dynamic_slice_in_dim(src_idx, first, group_size, 0)
        blocks = jnp.take(blocks_all, part_src, axis=0)
        if transpose:
            prod = jnp.einsum(
                "gab,gac->gbc", part_values, blocks, preferred_element_type=jnp.float32
            )
        else:
            prod = jnp.einsum(
                "gab,gbc->gac", part_values, blocks, preferred_element_type=jnp.float32
            )
        keep = (jnp.arange(group_size) + first < live).astype(jnp.float32)
        return acc.at[part_dest].add(prod * keep[:, None, None])

    start_acc = jnp.zeros((dest_tiles, side, width), jnp.float32)
    steps_used = values.shape[0] // group_size
    total = lax.fori_loop(0, steps_used, one_group, start_acc)
    return total.reshape(dest_tiles * side, width)


def body(features, weight, bias, grad_out, tile_rows, tile_cols, tile_counts, tile_values):
    values = tile_values[0, 0]
    rows_idx = tile_rows[0, 0]
    cols_idx = tile_cols[0, 0]
    live = tile_counts[0, 0]
    side = values.shape[-1]
    share = features.shape[0]
    row_tiles = share * lax.axis_size("col") // side
    col_tiles = share * lax.axis_size("row") // side
    mixed = jnp.dot(features, weight, preferred_element_type=jnp.float32).astype(jnp.bfloat16)
    column_block = lax.all_gather(mixed, "row", axis=0, tiled=True)
    partial_value = accumulate(values, rows_idx, cols_idx, live, column_block, row_tiles, False)
    pre_share = (
        lax.psum_scatter(
            partial_value.astype(jnp.bfloat16), "col", scatter_dimension=0, tiled=True
        ).astype(jnp.float32)
        + bias[None, :]
    )
    grad_share = (grad_out.astype(jnp.float32) * elu_slope(pre_share)).astype(jnp.bfloat16)
    grad_block = lax.all_gather(grad_share, "col", axis=0, tiled=True)
    output = elu_value(pre_share).astype(jnp.bfloat16)
    back = accumulate(values, cols_idx, rows_idx, live, grad_block, col_tiles, True)
    grad_mixed = lax.psum_scatter(back.astype(jnp.bfloat16), "row", scatter_dimension=0, tiled=True)
    grad_features = lax.dot_general(
        grad_mixed, weight, (((1,), (1,)), ((), ())), preferred_element_type=jnp.float32
    ).astype(jnp.bfloat16)
    weight_term = lax.dot_general(
        features, grad_mixed, (((0,), (0,)), ((), ())), preferred_element_type=jnp.float32
    )
    bias_term = jnp.sum(grad_share.astype(jnp.float32), axis=0)
    grad_weight, grad_bias = lax.psum((weight_term, bias_term), ("row", "col"))
    return (output, grad_features, grad_weight, grad_bias)


def solution(mesh):
    placed = (
        P(("col", "row"), None),
        P(),
        P(),
        P(("row", "col"), None),
        P("row", "col", None),
        P("row", "col", None),
        P("row", "col"),
        P("row", "col", None, None, None),
    )
    return jax.shard_map(
        body,
        mesh=mesh,
        in_specs=placed,
        out_specs=(P(("row", "col"), None), P(("col", "row"), None), P(), P()),
        check_vma=False,
    )
```

profile of v0, /device:TPU:0, one launch (start us, length us, event | category | flops | bytes accessed | tf_op | source)
XLA Modules:
  0.0 400.0 jit_solution(8134680617324430991)
XLA Ops:
  9.1 15.6 %all_gather.6 = bf16[512,256]{1,0:T(8,128)(2,1)S(1)} all-gather(bf16[128,256]{1,0:T(8,128)(2,1)S(1)} %convolution_convert_fusion.1), channel_id=1, replica_groups=mesh['row'=4,'col'=8] {'row'}, dimensions={0}, use_global_device_ids=true | all-gather | bytes 327680 | tf_op jit(solution)/shard_map/all_gather | solution.py:56
  24.8 86.4 %while.26 = (s32[]{:T(128)}, f32[8,128,256]{2,1,0:T(8,128)S(1)}, s32[128]{0:T(128)}, bf16[128,128,128]{2,1,0:T(8,128)(2,1)}, s32[128]{0:T(128)}, /*index=5*/bf16...) while((s32[]{:T(128)}, f32[8,128,256]{2,1,0:T(8,128)S(1)}, ...), condition=%wide.region_2.3_spmd, body=%wide.region_0.2_spmd.sunk | while | flops 67896424 | bytes 6033887 | solution.py:42
  24.8 1.4 compare_and_fusion.4
  28.9 1.3 scatter_fusion
  30.2 1.4 compare_and_fusion.4
  32.2 1.3 convolution_multiply_fusion.4
  34.3 1.3 scatter_fusion
  35.6 1.4 compare_and_fusion.4
  41.0 1.4 compare_and_fusion.4
  43.0 1.3 convolution_multiply_fusion.4
  45.1 1.3 scatter_fusion
  46.4 1.4 compare_and_fusion.4
  50.5 1.3 scatter_fusion
  51.8 1.4 compare_and_fusion.4
  53.8 1.3 convolution_multiply_fusion.4
  55.9 1.3 scatter_fusion
  57.2 1.4 compare_and_fusion.4
  59.2 1.3 convolution_multiply_fusion.4
  61.3 1.3 scatter_fusion
  62.6 1.4 compare_and_fusion.4
  68.0 1.4 compare_and_fusion.4
  72.1 1.3 scatter_fusion
  73.4 1.4 compare_and_fusion.4
  77.5 1.3 scatter_fusion
  78.8 1.4 compare_and_fusion.4
  82.9 1.3 scatter_fusion
  84.2 1.4 compare_and_fusion.4
  88.3 1.3 scatter_fusion
  89.6 1.4 compare_and_fusion.4
  95.0 1.4 compare_and_fusion.4
  100.4 1.4 compare_and_fusion.4
  102.4 1.3 convolution_multiply_fusion.4
  105.8 1.4 compare_and_fusion.4
  109.8 1.3 scatter_fusion
  112.2 6.4 %copy.12 = bf16[1,1,128,128,128]{3,4,2,1,0:T(8,128)(2,1)} copy(bf16[1,1,128,128,128]{4,3,2,1,0:T(8,128)(2,1)} %bitcast.20) | data formatting | bytes 8388608 | tf_op args[7]
  118.6 29.3 %reduce-scatter.3.cloned.1.call-done = bf16[128,256]{1,0:T(8,128)(2,1)} async-done(((bf16[1024,256]{1,0:T(8,128)(2,1)}), bf16[128,256]{1,0:T(8,128)(2,1)}) %reduce-scatter.3.cloned.1.call-update) | async-done | bytes 65552 | tf_op jit(solution)/shard_map/reduce_scatter | solution.py:59
  147.8 1.6 convert_reduce_fusion
  149.4 9.8 %all_gather.7 = bf16[1024,256]{1,0:T(8,128)(2,1)S(1)} all-gather(bf16[128,256]{1,0:T(8,128)(2,1)S(1)} %get-tuple-element.298), channel_id=1, replica_groups=mesh['row'=4,'col'=8] {'col'}, dimensions={0}, use_global_device_ids=true | all-gather | bytes 589824 | tf_op jit(solution)/shard_map/all_gather | solution.py:65
  159.3 65.2 %while.27 = (s32[]{:T(128)}, f32[4,128,256]{2,1,0:T(8,128)S(1)}, s32[128]{0:T(128)S(1)}, bf16[128,128,128]{1,2,0:T(8,128)(2,1)}, s32[128]{0:T(128)S(1)}, /*index...) while((s32[]{:T(128)}, f32[4,128,256]{2,1,0:T(8,128)S(1)}, ...), condition=%wide.region_6.7_spmd, body=%wide.region_4.6_spmd.sunk | while | flops 67896424 | bytes 6033887 | solution.py:42
  172.9 1.3 convolution_multiply_fusion.5
  176.9 1.3 convolution_multiply_fusion.5
  181.0 1.3 convolution_multiply_fusion.5
  217.7 1.3 convolution_multiply_fusion.5
  225.3 39.4 %psum.15 = f32[256]{0:T(256)} all-reduce(f32[256]{0:T(256)S(1)} %get-tuple-element.297), channel_id=1, replica_groups=mesh['row'=4,'col'=8] {'row','col'}, use_global_device_ids=true, to_apply=%region_10.11 | all-reduce | flops 256 | bytes 2048 | tf_op jit(solution)/shard_map/psum | solution.py:76
  264.7 1.8 convolution_bitcast_fusion
  266.5 1.7 convolution_convert_fusion
  268.1 123.6 %all-reduce.2.cloned.1.call-done = f32[256,256]{0,1:T(8,128)} async-done(((f32[256,256]{0,1:T(8,128)}), f32[256,256]{0,1:T(8,128)}) %all-reduce.2.cloned.1.call-update) | async-done | bytes 262160 | tf_op jit(solution)/shard_map/psum | solution.py:76
  391.7 1.8 copy.14
  (180 shorter events, 105.2 us)
Async XLA Ops:
  7.2 0.9 copy-start
  7.2 140.7 %reduce-scatter.3.cloned.1.call-start = ((), (), s32[]{:S(2)}) async-start(), calls=%async_computation.2 | async-start | bytes 589824 | tf_op jit(solution)/shard_map/reduce_scatter | solution.py:59
  112.1 35.8 %copy-start.2 = (bf16[128,256]{1,0:T(8,128)(2,1)S(1)}, bf16[128,256]{1,0:T(8,128)(2,1)}, u32[]{:S(2)}) copy-start(bf16[128,256]{1,0:T(8,128)(2,1)} %param.15) | copy-start | bytes 196612
  112.1 35.8 %copy-start.5 = (f32[256]{0:T(256)S(1)}, f32[256]{0:T(256)}, u32[]{:S(2)}) copy-start(f32[256]{0:T(256)} %param.14) | copy-start | bytes 3076
  112.1 47.1 %copy-start.3 = (s32[128]{0:T(128)S(1)}, s32[128]{0:T(128)}, u32[]{:S(2)}) copy-start(s32[128]{0:T(128)} %get-tuple-element.479) | copy-start | bytes 1540
  112.1 47.1 %copy-start.4 = (s32[128]{0:T(128)S(1)}, s32[128]{0:T(128)}, u32[]{:S(2)}) copy-start(s32[128]{0:T(128)} %get-tuple-element.480) | copy-start | bytes 1540
  112.1 152.6 %reduce-scatter.5.cloned.1.call-start = ((), (), s32[]{:S(2)}) async-start(), calls=%async_computation.3 | async-start | bytes 327680 | tf_op jit(solution)/shard_map/reduce_scatter | solution.py:68
  159.2 105.4 %copy-start.1 = (bf16[128,256]{1,0:T(8,128)(2,1)S(1)}, bf16[128,256]{1,0:T(8,128)(2,1)}, u32[]{:S(2)}) copy-start(bf16[128,256]{1,0:T(8,128)(2,1)} %param.12) | copy-start | bytes 196612
  225.3 166.5 %all-reduce.2.cloned.1.call-start = ((), (), s32[]{:S(2)}) async-start(), calls=%async_computation.4 | async-start | bytes 524288 | tf_op jit(solution)/shard_map/psum | solution.py:76
Sparse Core Ops, SparseCore 0:
  112.2 35.6 reduce-scatter.2
  225.4 19.6 reduce-scatter.4
  266.6 125.1 all-reduce.1
where the time goes:
time: 402 us; the launch traced here: 400 us
  waiting for transfers between devices  153 us (38%)
  other arithmetic  92.4 us (23%)
  blocking collectives  64.8 us (16%)
  matrix products  46.7 us (12%)
  local copies, waits for them, and re-layouts  27.8 us (7%)
  between operations  13.9 us (3%)
    psum x1, waiting for transfers between devices, body(): grad_weight, grad_bias = lax.psum((weight_term, bias_term), ('row', 'col'))  124 us
    scatter-add x32, other arithmetic, one_group(): return acc.at[part_dest].add(prod * keep[:, None, None])  42.2 us
    psum x1, blocking collectives, body(): grad_weight, grad_bias = lax.psum((weight_term, bias_term), ('row', 'col'))  39.4 us
    and x32, other arithmetic, one_group(): blocks = jnp.take(blocks_all, part_src, axis=0)  33.8 us
    reduce_scatter x1, waiting for transfers between devices, body(): lax.psum_scatter(partial_value.astype(jnp.bfloat16), 'col', scatter_dimen...  29.3 us
    dot_general x16, matrix products, one_group(): jnp.einsum('gab,gbc->gac', part_values, blocks, preferred_element_type=jn...  21.1 us
    dot_general x16, matrix products, one_group(): jnp.einsum('gab,gac->gbc', part_values, blocks, preferred_element_type=jn...  21.1 us
    gather x32, local copies, waits for them, and re-layouts, one_group(): blocks = jnp.take(blocks_all, part_src, axis=0)  18.6 us
  transfers between devices with their start and end apart: 3, of which 2 were waited for; matrix products, arithmetic and copies ran while one was open for 2% of the time, Pallas kernels for 0%

commit v1 on v0

v1 whole, which is shorter than its diff:
```python
import functools

import jax
import jax.numpy as jnp
from jax import lax
from jax.experimental import pallas as pl
from jax.experimental.pallas import tpu as pltpu
from jax.sharding import PartitionSpec as P

MESH = pl.DeviceIdType.MESH
CHUNKS = 4
F32 = jnp.float32
BF16 = jnp.bfloat16


def each(n, step):
    if n <= 8:
        for i in range(n):
            step(i)
    else:
        lax.fori_loop(0, n, lambda i, _: (step(i), 0)[1], 0)


def kernel(
    n_row, n_col, row_tiles, col_tiles,
    feat_ref, weight_ref, bias_ref, gout_ref, rows_ref, cols_ref, count_ref, values_ref,
    out_ref, gfeat_ref, gw_ref, gb_ref,
    vals, seq, dense, dense_t, feat_all, feat_t, mixed, part_send, part_recv, grad_all,
    back_send, back_recv, gw_send, gw_recv, gwz_recv, gw_all, gb_recv, idx_v, idx_s,
    val_sem, idx_sem, f_send, f_recv, p_send, p_recv, g_send, g_recv, b_send, b_recv,
    w_send, w_recv, z_send, z_recv, a_send, a_recv, s_send, s_recv,
):
    my_r = lax.axis_index("row")
    my_c = lax.axis_index("col")
    slots, side = vals.shape[0], vals.shape[1]
    share, width = feat_ref.shape
    per = slots // CHUNKS
    chunk = width // n_col

    def row_peer(d):
        return lax.rem(my_r + d, n_row)

    def row_from(d):
        return lax.rem(my_r + n_row - d, n_row)

    def col_peer(d):
        return lax.rem(my_c + d, n_col)

    def col_from(d):
        return lax.rem(my_c + n_col - d, n_col)

    def to_row(src, dst, send, recv, d):
        return pltpu.make_async_remote_copy(
            src_ref=src, dst_ref=dst, send_sem=send.at[d], recv_sem=recv.at[d],
            device_id=(row_peer(d), my_c), device_id_type=MESH)

    def to_col(src, dst, send, recv, d):
        return pltpu.make_async_remote_copy(
            src_ref=src, dst_ref=dst, send_sem=send.at[d], recv_sem=recv.at[d],
            device_id=(my_r, col_peer(d)), device_id_type=MESH)

    def fetch(q):
        return pltpu.make_async_copy(
            values_ref.at[pl.ds(q * per, per)], vals.at[pl.ds(q * per, per)], val_sem.at[q])

    for q in range(CHUNKS):
        fetch(q).start()

    barrier = pltpu.get_barrier_semaphore()
    for d in range(1, n_row):
        pl.semaphore_signal(barrier, inc=1, device_id=(row_peer(d), my_c), device_id_type=MESH)
    for d in range(1, n_col):
        pl.semaphore_signal(barrier, inc=1, device_id=(my_r, col_peer(d)), device_id_type=MESH)

    tiles = row_tiles * col_tiles
    lane = lax.broadcasted_iota(jnp.int32, (slots, slots), 1)
    sub = lax.broadcasted_iota(jnp.int32, (slots, slots), 0)
    live = lane < count_ref[0, 0]
    key = jnp.where(
        live, jnp.broadcast_to(rows_ref[...] * col_tiles + cols_ref[...], (slots, slots)), tiles)
    key_t = key.T
    ahead = (key_t < key) | ((key_t == key) & (sub < lane))
    rank = jnp.sum(ahead.astype(jnp.int32), axis=0, keepdims=True)
    hit = jnp.broadcast_to(rank, (slots, slots)).T == lane
    idx_v[0:1, :] = jnp.sum(jnp.where(hit, sub, 0), axis=0, keepdims=True)
    idx_v[1:2, :] = jnp.sum(jnp.where(hit, key_t, 0), axis=0, keepdims=True)
    for q in range(-(-tiles // slots)):
        upto = (key_t <= lane + q * slots).astype(jnp.int32)
        idx_v[2 + q : 3 + q, :] = jnp.sum(upto, axis=0, keepdims=True)
    idx_copy = pltpu.make_async_copy(idx_v, idx_s, idx_sem)
    idx_copy.start()

    pl.semaphore_wait(barrier, n_row + n_col - 2)

    def feat_copy(d):
        return to_row(feat_ref, feat_all.at[my_r], f_send, f_recv, d)

    for d in range(1, n_row):
        feat_copy(d).start()
    feat_all[my_r] = feat_ref[...]

    idx_copy.wait()
    for q in range(CHUNKS):
        fetch(q).wait()

    def add_slot(i, acc):
        same = (i > 0) & (idx_s[1, i] == idx_s[1, jnp.maximum(i - 1, 0)])
        keep = jnp.where(same, 1.0, 0.0).astype(F32)
        acc = acc * keep + vals[idx_s[0, i]].astype(F32)
        seq[i] = acc.astype(BF16)
        return acc

    lax.fori_loop(0, slots, add_slot, jnp.zeros((side, side), F32), unroll=4)

    def dense_tile(r, c):
        k = r * col_tiles + c
        before = jnp.maximum(k - 1, 0)
        end = idx_s[2 + k // slots, lax.rem(k, slots)]
        start = jnp.where(k > 0, idx_s[2 + before // slots, lax.rem(before, slots)], 0)
        some = jnp.where(end > start, 1.0, 0.0).astype(F32)
        return (seq[jnp.maximum(end - 1, 0)].astype(F32) * some).astype(BF16)

    def place(r, _):
        for c in range(col_tiles):
            dense[pl.ds(pl.multiple_of(r * side, side), side), c * side : (c + 1) * side] = (
                dense_tile(r, c))
        return 0

    lax.fori_loop(0, row_tiles, place, 0)

    def mix(i):
        mixed[pl.ds(i * share, share), :] = jnp.dot(
            feat_all[i], weight_ref[...], preferred_element_type=F32).astype(BF16)

    mix(my_r)

    for d in range(1, n_row):
        feat_copy(d).wait_recv()
        mix(row_from(d))

    def part_copy(d):
        return to_col(part_send.at[d], part_recv.at[d], p_send, p_recv, d)

    def forward(j):
        return jnp.dot(
            dense[pl.ds(pl.multiple_of(j * share, share), share), :], mixed[...],
            preferred_element_type=F32)

    def forward_send(i):
        d = i + 1
        part_send[d] = forward(col_peer(d)).astype(BF16)
        part_copy(d).start()

    each(n_col - 1, forward_send)
    pre = forward(my_c) + bias_ref[...]

    def turn(r, _):
        for c in range(col_tiles):
            tile = dense[pl.ds(pl.multiple_of(r * side, side), side), c * side : (c + 1) * side]
            dense_t[c * side : (c + 1) * side, pl.ds(pl.multiple_of(r * side, side), side)] = (
                tile.astype(F32).T.astype(BF16))
        return 0

    lax.fori_loop(0, row_tiles, turn, 0)

    def turn_feat(i, _):
        feat_t[:, pl.ds(pl.multiple_of(i * share, share), share)] = (
            feat_all[i].astype(F32).T.astype(BF16))
        return 0

    lax.fori_loop(0, n_row, turn_feat, 0)

    for d in range(1, n_col):
        part_copy(d).wait_recv()
        pre = pre + part_recv[d].astype(F32)

    low = jnp.exp(jnp.minimum(pre, 0.0))
    grad = (gout_ref[...].astype(F32) * jnp.where(pre > 0, 1.0, low)).astype(BF16)
    my_rows = pl.ds(pl.multiple_of(my_c * share, share), share)
    grad_all[my_rows, :] = grad

    def grad_copy(d):
        return to_col(grad_all.at[my_rows], grad_all.at[my_rows], g_send, g_recv, d)

    for d in range(1, n_col):
        grad_copy(d).start()
    out_ref[...] = jnp.where(pre > 0, pre, low - 1.0).astype(BF16)
    for d in range(1, n_col):
        grad_copy(d).wait_recv()

    def back_copy(d):
        return to_row(back_send.at[row_peer(d)], back_recv.at[d], b_send, b_recv, d)

    def backward(i):
        return jnp.dot(
            dense_t[pl.ds(pl.multiple_of(i * share, share), share), :], grad_all[...],
            preferred_element_type=F32)

    def backward_send(i):
        d = i + 1
        back_send[row_peer(d)] = backward(row_peer(d)).astype(BF16)
        back_copy(d).start()

    each(n_row - 1, backward_send)
    total = backward(my_r)
    back_send[my_r] = total.astype(BF16)

    def gw_copy(d):
        return to_col(gw_send.at[col_peer(d)], gw_recv.at[d], w_send, w_recv, d)

    term = jnp.dot(
        feat_t[...], back_send[...].reshape(n_row * share, width), preferred_element_type=F32)
    gw_send[...] = term.astype(gw_send.dtype).reshape(n_col, chunk, width)
    for d in range(1, n_col):
        gw_copy(d).start()

    def gb_copy(d):
        return to_row(gb_recv.at[my_r], gb_recv.at[my_r], s_send, s_recv, d)

    ones = jnp.ones((16, n_col * share), BF16)
    gb_recv[my_r] = jnp.dot(ones, grad_all[...], preferred_element_type=F32)[:8]
    for d in range(1, n_row):
        gb_copy(d).start()

    gw_sum = gw_send[my_c].astype(F32)
    for d in range(1, n_col):
        gw_copy(d).wait_recv()
        gw_sum = gw_sum + gw_recv[d].astype(F32)

    def gwz_copy(d):
        return to_row(gwz_recv.at[my_r], gwz_recv.at[my_r], z_send, z_recv, d)

    gwz_recv[my_r] = gw_sum.astype(gw_send.dtype)
    for d in range(1, n_row):
        gwz_copy(d).start()

    for d in range(1, n_row):
        back_copy(d).wait_recv()
        total = total + back_recv[d].astype(F32)
    gfeat_ref[...] = lax.dot_general(
        total.astype(BF16), weight_ref[...], (((1,), (1,)), ((), ())),
        preferred_element_type=F32).astype(BF16)

    for d in range(1, n_row):
        gwz_copy(d).wait_recv()
    whole = gwz_recv[0].astype(F32)
    for i in range(1, n_row):
        whole = whole + gwz_recv[i].astype(F32)

    def all_copy(d):
        return to_col(gw_all.at[my_c], gw_all.at[my_c], a_send, a_recv, d)

    gw_all[my_c] = whole.astype(gw_all.dtype)
    for d in range(1, n_col):
        all_copy(d).start()

    for d in range(1, n_row):
        gb_copy(d).wait_recv()
    gb = gb_recv[0]
    for i in range(1, n_row):
        gb = gb + gb_recv[i]
    gb_ref[...] = gb[0:1]

    for d in range(1, n_row):
        feat_copy(d).wait_send()
        back_copy(d).wait_send()
        gwz_copy(d).wait_send()
        gb_copy(d).wait_send()
    for d in range(1, n_col):
        part_copy(d).wait_send()
        grad_copy(d).wait_send()
        gw_copy(d).wait_send()
    for d in range(1, n_col):
        all_copy(d).wait_recv()
    gw_ref[...] = gw_all[...].astype(F32).reshape(width, width)
    for d in range(1, n_col):
        all_copy(d).wait_send()


def body(n_row, n_col, features, weight, bias, grad_out, tile_rows, tile_cols, tile_counts, tile_values):
    values = tile_values[0, 0]
    slots, side = values.shape[0], values.shape[1]
    share, width = features.shape
    row_tiles = share * n_col // side
    col_tiles = share * n_row // side
    chunk = width // n_col
    gw_type = BF16 if chunk % 16 == 0 else F32
    index_rows = -(-(2 + -(-(row_tiles * col_tiles) // slots)) // 8) * 8
    vmem = pl.BlockSpec(memory_space=pltpu.VMEM)
    smem = pl.BlockSpec(memory_space=pltpu.SMEM)
    dma = pltpu.SemaphoreType.DMA
    row_sem, col_sem = dma((n_row,)), dma((n_col,))
    out, gfeat, gw, gb = pl.pallas_call(
        functools.partial(kernel, n_row, n_col, row_tiles, col_tiles),
        out_shape=(
            jax.ShapeDtypeStruct((share, width), BF16),
            jax.ShapeDtypeStruct((share, width), BF16),
            jax.ShapeDtypeStruct((width, width), F32),
            jax.ShapeDtypeStruct((1, width), F32),
        ),
        in_specs=[vmem] * 6 + [smem, pl.BlockSpec(memory_space=pl.ANY)],
        out_specs=(vmem, vmem, vmem, vmem),
        scratch_shapes=[
            pltpu.VMEM((slots, side, side), BF16),
            pltpu.VMEM((slots, side, side), BF16),
            pltpu.VMEM((row_tiles * side, col_tiles * side), BF16),
            pltpu.VMEM((col_tiles * side, row_tiles * side), BF16),
            pltpu.VMEM((n_row, share, width), BF16),
            pltpu.VMEM((width, n_row * share), BF16),
            pltpu.VMEM((n_row * share, width), BF16),
            pltpu.VMEM((n_col, share, width), BF16),
            pltpu.VMEM((n_col, share, width), BF16),
            pltpu.VMEM((n_col * share, width), BF16),
            pltpu.VMEM((n_row, share, width), BF16),
            pltpu.VMEM((n_row, share, width), BF16),
            pltpu.VMEM((n_col, chunk, width), gw_type),
            pltpu.VMEM((n_col, chunk, width), gw_type),
            pltpu.VMEM((n_row, chunk, width), gw_type),
            pltpu.VMEM((n_col, chunk, width), gw_type),
            pltpu.VMEM((n_row, 8, width), F32),
            pltpu.VMEM((index_rows, slots), jnp.int32),
            pltpu.SMEM((index_rows, slots), jnp.int32),
            dma((CHUNKS,)), dma(()),
            row_sem, row_sem, col_sem, col_sem, col_sem, col_sem, row_sem, row_sem,
            col_sem, col_sem, row_sem, row_sem, col_sem, col_sem, row_sem, row_sem,
        ],
        compiler_params=pltpu.CompilerParams(
            collective_id=0, has_side_effects=True, vmem_limit_bytes=60 * 2**20),
        cost_estimate=pl.CostEstimate(
            flops=4 * row_tiles * col_tiles * side * side * width,
            bytes_accessed=2 * slots * side * side, transcendentals=share * width),
    )(features, weight, bias[None, :], grad_out, tile_rows[0], tile_cols[0], tile_counts, values)
    return out, gfeat, gw, gb[0]


def solution(mesh):
    placed = (
        P(("col", "row"), None),
        P(),
        P(),
        P(("row", "col"), None),
        P("row", "col", None),
        P("row", "col", None),
        P("row", "col"),
        P("row", "col", None, None, None),
    )
    return jax.shard_map(
        functools.partial(body, mesh.shape["row"], mesh.shape["col"]),
        mesh=mesh,
        in_specs=placed,
        out_specs=(P(("row", "col"), None), P(("col", "row"), None), P(), P()),
        check_vma=False,
    )
```

time: 402 us -> 49.9 us (0.12)
  waiting for transfers between devices: 153 us -> 0 us
  other arithmetic: 92.4 us -> 0 us
  blocking collectives: 64.8 us -> 0 us
  matrix products: 46.7 us -> 0 us
  Pallas kernels: 0 us -> 42.5 us
  local copies, waits for them, and re-layouts: 27.8 us -> 5.81 us
  between operations: 13.9 us -> 1.29 us
    psum x1 -> x0, waiting for transfers between devices: 124 us -> none  [body(): grad_weight, grad_bias = lax.psum((weight_term, bias_term), ('row', 'col'))]
    dot_general x35 -> x0, matrix products: 46.7 us -> none  [the longest x16 21.1 us: one_group(): jnp.einsum('gab,gbc->gac', part_values, blocks, preferred_element_type=jn...]
    pallas_call x0 -> x1, Pallas kernels: none -> 42.5 us  [body(): pl.pallas_call(functools.partial(kernel, n_row, n_col, row_tiles, col_til...]
    scatter-add x32 -> x0, other arithmetic: 42.2 us -> none  [one_group(): return acc.at[part_dest].add(prod * keep[:, None, None])]
    psum x1 -> x0, blocking collectives: 39.4 us -> none  [body(): grad_weight, grad_bias = lax.psum((weight_term, bias_term), ('row', 'col'))]
    and x32 -> x0, other arithmetic: 33.8 us -> none  [one_group(): blocks = jnp.take(blocks_all, part_src, axis=0)]
    reduce_scatter x2 -> x0, waiting for transfers between devices: 29.3 us -> none  [the longest x1 29.3 us: body(): lax.psum_scatter(partial_value.astype(jnp.bfloat16), 'col', scatter_dimen...]
    all_gather x2 -> x0, blocking collectives: 25.4 us -> none  [the longest x1 15.6 us: body(): column_block = lax.all_gather(mixed, 'row', axis=0, tiled=True)]
  transfers between devices with their start and end apart: 3 -> 0, of which waited for: 2 -> 0; matrix products, arithmetic and copies ran while one was open for 2% -> 0% of each run, Pallas kernels for 0% -> 0%
where the time goes in v1:
time: 49.9 us; the launch traced here: 49.6 us
  Pallas kernels  42.5 us (85%)
  local copies, waits for them, and re-layouts  5.81 us (12%)
  between operations  1.29 us (3%)
    pallas_call x1, Pallas kernels, body(): pl.pallas_call(functools.partial(kernel, n_row, n_col, row_tiles, col_til...  42.5 us
    unnamed x4, local copies, waits for them, and re-layouts  5.81 us

profile of v1, /device:TPU:0, one launch (start us, length us, event | category | flops | bytes accessed | tf_op | source)
XLA Modules:
  0.0 49.6 jit_solution(303775305076736415)
XLA Ops:
  1.3 42.5 %shard_map.111 = (bf16[128,256]{1,0:T(8,128)(2,1)}, bf16[128,256]{1,0:T(8,128)(2,1)}, f32[256,256]{1,0:T(8,128)}, f32[1,256]{1,0:T(1,128)}) custom-call(bf16[128,256]{1,0:T(8,128)(2,1)} %feat_ref.1, bf16[256,256]{1,0:T(8,128)(2,1)} %weight_ref.1, f32[1,256]{1,0:T(1,128)} %bitcast.6, bf16[128,256]{1,0:T(8,128)(2,1)} %gout_ref.1, s32[1,128]{1,0:T(1,128)} %bitcast.8, ...), custom_call_target="tpu_custom_call" | custom-call | flops 536870912 | bytes 4194304 | tf_op jit(solution)/shard_map/pallas_call | solution.py:293
  43.8 1.5 %copy.17 = bf16[128,256]{1,0:T(8,128)(2,1)} copy(bf16[128,256]{1,0:T(8,128)(2,1)} %get-tuple-element.16) | data formatting | bytes 131072
  45.3 1.5 %copy.18 = bf16[128,256]{1,0:T(8,128)(2,1)} copy(bf16[128,256]{1,0:T(8,128)(2,1)} %get-tuple-element.17) | data formatting | bytes 131072
  46.8 1.7 %copy.19 = f32[256,256]{1,0:T(8,128)} copy(f32[256,256]{1,0:T(8,128)} %get-tuple-element.18) | data formatting | bytes 524288
  48.4 1.2 %copy.20 = f32[256]{0:T(256)} copy(f32[256]{0:T(256)} %bitcast.7) | data formatting | bytes 2048

commit v2 on v1

v2 whole, which is shorter than its diff:
```python
import functools
import math

import jax
import jax.numpy as jnp
from jax import lax
from jax.experimental import pallas as pl
from jax.experimental.pallas import tpu as pltpu
from jax.sharding import PartitionSpec as P

MESH = pl.DeviceIdType.MESH
CHUNKS = 4
F32 = jnp.float32
BF16 = jnp.bfloat16


def each(n, step):
    if n <= 8:
        for i in range(n):
            step(i)
    else:
        lax.fori_loop(0, n, lambda i, _: (step(i), 0)[1], 0)


def kernel(
    n_row, n_col, row_tiles, col_tiles,
    feat_ref, weight_ref, bias_ref, gout_ref, rows_ref, cols_ref, count_ref, values_ref,
    out_ref, gmix_ref, gw_ref, gb_ref,
    vals, seq, dense, dense_t, feat_all, pair_send, pair_recv, part_send, part_recv, grad_all,
    back_send, back_recv, gw_send, gw_recv, gwz_recv, gw_all, gb_recv, idx_v, idx_s,
    val_sem, idx_sem, f_send, f_recv, p_send, p_recv, q_send, q_recv, g_send, g_recv,
    h_send, h_recv, b_send, b_recv,
    w_send, w_recv, z_send, z_recv, a_send, a_recv, s_send, s_recv,
):
    my_r = lax.axis_index("row")
    my_c = lax.axis_index("col")
    n_chip = n_col // 2
    core, chip = lax.rem(my_c, 2), my_c // 2
    sibling = my_c + 1 - 2 * core
    slots, side = vals.shape[0], vals.shape[1]
    share, width = feat_ref.shape
    per = slots // CHUNKS
    chunk = width // n_col

    def row_peer(d):
        return lax.rem(my_r + d, n_row)

    def col_peer(d):
        return lax.rem(my_c + d, n_col)

    def chip_peer(d):
        return 2 * lax.rem(chip + d, n_chip) + core

    def to_row(src, dst, send, recv, d):
        return pltpu.make_async_remote_copy(
            src_ref=src, dst_ref=dst, send_sem=send.at[d], recv_sem=recv.at[d],
            device_id=(row_peer(d), my_c), device_id_type=MESH)

    def to_col(src, dst, send, recv, d, peer):
        return pltpu.make_async_remote_copy(
            src_ref=src, dst_ref=dst, send_sem=send.at[d], recv_sem=recv.at[d],
            device_id=(my_r, peer), device_id_type=MESH)

    def fetch(q):
        return pltpu.make_async_copy(
            values_ref.at[pl.ds(q * per, per)], vals.at[pl.ds(q * per, per)], val_sem.at[q])

    for q in range(CHUNKS):
        fetch(q).start()

    barrier = pltpu.get_barrier_semaphore()
    for d in range(1, n_row):
        pl.semaphore_signal(barrier, inc=1, device_id=(row_peer(d), my_c), device_id_type=MESH)
    for d in range(1, n_col):
        pl.semaphore_signal(barrier, inc=1, device_id=(my_r, col_peer(d)), device_id_type=MESH)

    tiles = row_tiles * col_tiles
    lane = lax.broadcasted_iota(jnp.int32, (slots, slots), 1)
    sub = lax.broadcasted_iota(jnp.int32, (slots, slots), 0)
    live = lane < count_ref[0, 0]
    key = jnp.where(
        live, jnp.broadcast_to(rows_ref[...] * col_tiles + cols_ref[...], (slots, slots)), tiles)
    key_t = key.T
    ahead = (key_t < key) | ((key_t == key) & (sub < lane))
    rank = jnp.sum(ahead.astype(jnp.int32), axis=0, keepdims=True)
    hit = jnp.broadcast_to(rank, (slots, slots)).T == lane
    idx_v[0:1, :] = jnp.sum(jnp.where(hit, sub, 0), axis=0, keepdims=True)
    idx_v[1:2, :] = jnp.sum(jnp.where(hit, key_t, 0), axis=0, keepdims=True)
    for q in range(-(-tiles // slots)):
        upto = (key_t <= lane + q * slots).astype(jnp.int32)
        idx_v[2 + q : 3 + q, :] = jnp.sum(upto, axis=0, keepdims=True)
    idx_copy = pltpu.make_async_copy(idx_v, idx_s, idx_sem)
    idx_copy.start()

    pl.semaphore_wait(barrier, n_row + n_col - 2)

    def feat_copy(d):
        return to_row(feat_ref, feat_all.at[my_r], f_send, f_recv, d)

    for d in range(1, n_row):
        feat_copy(d).start()
    feat_all[my_r] = feat_ref[...]

    idx_copy.wait()
    for q in range(CHUNKS):
        fetch(q).wait()

    def add_slot(i, acc):
        same = (i > 0) & (idx_s[1, i] == idx_s[1, jnp.maximum(i - 1, 0)])
        keep = jnp.where(same, 1.0, 0.0).astype(F32)
        acc = acc * keep + vals[idx_s[0, i]].astype(F32)
        seq[i] = acc.astype(BF16)
        return acc

    lax.fori_loop(0, slots, add_slot, jnp.zeros((side, side), F32), unroll=8)

    def dense_tile(r, c):
        k = r * col_tiles + c
        before = jnp.maximum(k - 1, 0)
        end = idx_s[2 + k // slots, lax.rem(k, slots)]
        start = jnp.where(k > 0, idx_s[2 + before // slots, lax.rem(before, slots)], 0)
        some = jnp.where(end > start, 1.0, 0.0).astype(F32)
        return (seq[jnp.maximum(end - 1, 0)].astype(F32) * some).astype(BF16)

    tiles_per = share // side

    def place(r, _):
        block, inner = r // tiles_per, lax.rem(r, tiles_per)
        at = (lax.rem(block, 2) * n_chip + block // 2) * tiles_per + inner
        for c in range(col_tiles):
            dense[pl.ds(pl.multiple_of(at * side, side), side), c * side : (c + 1) * side] = (
                dense_tile(r, c))
        return 0

    lax.fori_loop(0, row_tiles, place, 0)

    for d in range(1, n_row):
        feat_copy(d).wait_recv()

    def aggregate(block):
        return jnp.dot(
            dense[pl.ds(pl.multiple_of(block * share, share), share), :],
            feat_all[...].reshape(n_row * share, width), preferred_element_type=F32)

    def pair_copy(d):
        return to_col(pair_send.at[d], pair_recv.at[d], p_send, p_recv, d, sibling)

    def part_copy(d):
        return to_col(part_send.at[d], part_recv.at[d], q_send, q_recv, d, chip_peer(d))

    def pair_step(i):
        d = lax.rem(i + 1, n_chip)
        pair_send[d] = aggregate((1 - core) * n_chip + lax.rem(chip + d, n_chip)).astype(BF16)
        pair_copy(d).start()

    def part_step(i):
        d = i + 1
        mine = aggregate(core * n_chip + lax.rem(chip + d, n_chip))
        pair_copy(d).wait_recv()
        part_send[d] = (mine + pair_recv[d].astype(F32)).astype(BF16)
        part_copy(d).start()

    each(n_chip, pair_step)
    each(n_chip - 1, part_step)
    gathered = aggregate(core * n_chip + chip)
    pair_copy(0).wait_recv()
    gathered = gathered + pair_recv[0].astype(F32)

    def turn(r, _):
        for c in range(col_tiles):
            tile = dense[pl.ds(pl.multiple_of(r * side, side), side), c * side : (c + 1) * side]
            dense_t[c * side : (c + 1) * side, pl.ds(pl.multiple_of(r * side, side), side)] = (
                tile.astype(F32).T.astype(BF16))
        return 0

    lax.fori_loop(0, row_tiles, turn, 0)

    for d in range(1, n_chip):
        part_copy(d).wait_recv()
        gathered = gathered + part_recv[d].astype(F32)

    pre = jnp.dot(
        gathered.astype(BF16), weight_ref[...], preferred_element_type=F32) + bias_ref[...]
    low = jnp.exp(jnp.minimum(pre, 0.0))
    grad = (gout_ref[...].astype(F32) * jnp.where(pre > 0, 1.0, low)).astype(BF16)

    def rows_of(block):
        return grad_all.at[pl.ds(pl.multiple_of(block * share, share), share), :]

    mine_at = core * n_chip + chip
    grad_all[pl.ds(pl.multiple_of(mine_at * share, share), share), :] = grad

    def grad_copy(d):
        return to_col(rows_of(mine_at), rows_of(mine_at), g_send, g_recv, d, chip_peer(d))

    def hand_copy(d):
        at = core * n_chip + lax.rem(chip + n_chip - d, n_chip)
        return to_col(rows_of(at), rows_of(at), h_send, h_recv, d, sibling)

    for d in range(1, n_chip):
        grad_copy(d).start()
    hand_copy(0).start()
    out_ref[...] = jnp.where(pre > 0, pre, low - 1.0).astype(BF16)

    def gw_copy(d):
        return to_col(gw_send.at[col_peer(d)], gw_recv.at[d], w_send, w_recv, d, col_peer(d))

    term = jnp.dot(gathered.T.astype(BF16), grad, preferred_element_type=F32)
    gw_send[...] = term.astype(gw_send.dtype).reshape(n_col, chunk, width)
    for d in range(1, n_col):
        gw_copy(d).start()

    for d in range(1, n_chip):
        grad_copy(d).wait_recv()
        hand_copy(d).start()
    for d in range(n_chip):
        hand_copy(d).wait_recv()

    def back_copy(d):
        return to_row(back_send.at[d], back_recv.at[d], b_send, b_recv, d)

    def backward(i):
        return jnp.dot(
            dense_t[pl.ds(pl.multiple_of(i * share, share), share), :], grad_all[...],
            preferred_element_type=F32)

    def backward_send(i):
        d = i + 1
        back_send[d] = backward(row_peer(d)).astype(BF16)
        back_copy(d).start()

    each(n_row - 1, backward_send)

    gw_sum = gw_send[my_c].astype(F32)
    for d in range(1, n_col):
        gw_copy(d).wait_recv()
        gw_sum = gw_sum + gw_recv[d].astype(F32)

    def gwz_copy(d):
        return to_row(gwz_recv.at[my_r], gwz_recv.at[my_r], z_send, z_recv, d)

    gwz_recv[my_r] = gw_sum.astype(gw_send.dtype)
    for d in range(1, n_row):
        gwz_copy(d).start()

    def gb_copy(d):
        return to_row(gb_recv.at[my_r], gb_recv.at[my_r], s_send, s_recv, d)

    ones = jnp.ones((16, n_col * share), BF16)
    gb_recv[my_r] = jnp.dot(ones, grad_all[...], preferred_element_type=F32)[:8]
    for d in range(1, n_row):
        gb_copy(d).start()

    total = backward(my_r)

    for d in range(1, n_row):
        gwz_copy(d).wait_recv()
    whole = gwz_recv[0].astype(F32)
    for i in range(1, n_row):
        whole = whole + gwz_recv[i].astype(F32)

    def all_copy(d):
        return to_col(gw_all.at[my_c], gw_all.at[my_c], a_send, a_recv, d, col_peer(d))

    gw_all[my_c] = whole.astype(gw_all.dtype)
    for d in range(1, n_col):
        all_copy(d).start()

    for d in range(1, n_row):
        back_copy(d).wait_recv()
        total = total + back_recv[d].astype(F32)
    gmix_ref[...] = total.astype(BF16)

    for d in range(1, n_row):
        gb_copy(d).wait_recv()
    gb_ref[...] = gb_recv[...]

    for d in range(1, n_row):
        feat_copy(d).wait_send()
        back_copy(d).wait_send()
        gwz_copy(d).wait_send()
        gb_copy(d).wait_send()
    for d in range(n_chip):
        pair_copy(d).wait_send()
        hand_copy(d).wait_send()
    for d in range(1, n_chip):
        part_copy(d).wait_send()
        grad_copy(d).wait_send()
    for d in range(1, n_col):
        gw_copy(d).wait_send()
        all_copy(d).wait_recv()
    gw_ref[...] = gw_all[...]
    for d in range(1, n_col):
        all_copy(d).wait_send()


def finish(part_ref, gmix_ref, gwp_ref, gbp_ref, weight_ref, out_ref, gfeat_ref, gw_ref, gb_ref):
    out_ref[...] = part_ref[...]
    gfeat_ref[...] = lax.dot_general(
        gmix_ref[...], weight_ref[...], (((1,), (1,)), ((), ())),
        preferred_element_type=F32).astype(BF16)
    gw_ref[...] = gwp_ref[...].astype(F32).reshape(gw_ref.shape)
    gb = gbp_ref[0]
    for i in range(1, gbp_ref.shape[0]):
        gb = gb + gbp_ref[i]
    gb_ref[...] = gb[0:1]


def body(n_row, n_col, features, weight, bias, grad_out, tile_rows, tile_cols, tile_counts, tile_values):
    values = tile_values[0, 0]
    slots, side = values.shape[0], values.shape[1]
    share, width = features.shape
    row_tiles = share * n_col // side
    col_tiles = share * n_row // side
    chunk = width // n_col
    gw_type = BF16 if chunk % 16 == 0 else F32
    index_rows = -(-(2 + -(-(row_tiles * col_tiles) // slots)) // 8) * 8
    vmem = pl.BlockSpec(memory_space=pltpu.VMEM)
    smem = pl.BlockSpec(memory_space=pltpu.SMEM)
    dma = pltpu.SemaphoreType.DMA
    row_sem, col_sem, chip_sem = dma((n_row,)), dma((n_col,)), dma((n_col // 2,))
    buffers = [
        ((slots, side, side), BF16),
        ((slots, side, side), BF16),
        ((row_tiles * side, col_tiles * side), BF16),
        ((col_tiles * side, row_tiles * side), BF16),
        ((n_row, share, width), BF16),
        ((n_col // 2, share, width), BF16),
        ((n_col // 2, share, width), BF16),
        ((n_col // 2, share, width), BF16),
        ((n_col // 2, share, width), BF16),
        ((n_col * share, width), BF16),
        ((n_row, share, width), BF16),
        ((n_row, share, width), BF16),
        ((n_col, chunk, width), gw_type),
        ((n_col, chunk, width), gw_type),
        ((n_row, chunk, width), gw_type),
        ((n_col, chunk, width), gw_type),
        ((n_row, 8, width), F32),
        ((index_rows, slots), jnp.int32),
    ]
    held = sum(math.prod(shape) * jnp.dtype(kind).itemsize for shape, kind in buffers)
    out, gmix, gw, gb = pl.pallas_call(
        functools.partial(kernel, n_row, n_col, row_tiles, col_tiles),
        out_shape=(
            jax.ShapeDtypeStruct((share, width), BF16),
            jax.ShapeDtypeStruct((share, width), BF16),
            jax.ShapeDtypeStruct((n_col, chunk, width), gw_type),
            jax.ShapeDtypeStruct((n_row, 8, width), F32),
        ),
        in_specs=[vmem] * 6 + [smem, pl.BlockSpec(memory_space=pltpu.HBM)],
        out_specs=(vmem, vmem, vmem, vmem),
        scratch_shapes=[pltpu.VMEM(shape, kind) for shape, kind in buffers] + [
            pltpu.SMEM((index_rows, slots), jnp.int32),
            dma((CHUNKS,)), dma(()),
            row_sem, row_sem, chip_sem, chip_sem, chip_sem, chip_sem, chip_sem, chip_sem,
            chip_sem, chip_sem, row_sem, row_sem,
            col_sem, col_sem, row_sem, row_sem, col_sem, col_sem, row_sem, row_sem,
        ],
        compiler_params=pltpu.CompilerParams(
            collective_id=0, has_side_effects=True,
            vmem_limit_bytes=min(60 * 2**20, held + 12 * 2**20)),
        cost_estimate=pl.CostEstimate(
            flops=4 * row_tiles * col_tiles * side * side * width,
            bytes_accessed=2 * slots * side * side, transcendentals=share * width),
    )(features, weight, bias[None, :], grad_out, tile_rows[0], tile_cols[0], tile_counts, values)
    out, gfeat, gw, gb = pl.pallas_call(
        finish,
        out_shape=(
            jax.ShapeDtypeStruct((share, width), BF16),
            jax.ShapeDtypeStruct((share, width), BF16),
            jax.ShapeDtypeStruct((width, width), F32),
            jax.ShapeDtypeStruct((1, width), F32),
        ),
        in_specs=[vmem] * 5,
        out_specs=(vmem, vmem, vmem, vmem),
    )(out, gmix, gw, gb, weight)
    return out, gfeat, gw, gb[0]


def solution(mesh):
    placed = (
        P(("col", "row"), None),
        P(),
        P(),
        P(("row", "col"), None),
        P("row", "col", None),
        P("row", "col", None),
        P("row", "col"),
        P("row", "col", None, None, None),
    )
    return jax.shard_map(
        functools.partial(body, mesh.shape["row"], mesh.shape["col"]),
        mesh=mesh,
        in_specs=placed,
        out_specs=(P(("row", "col"), None), P(("col", "row"), None), P(), P()),
        check_vma=False,
    )
```

time: 49.9 us -> 51.5 us (1.032)
  local copies, waits for them, and re-layouts: 5.81 us -> 9.23 us
  Pallas kernels: 42.5 us -> 40.6 us
    pallas_call x1, Pallas kernels: 42.5 us -> 38.7 us  [body(): pl.pallas_call(functools.partial(kernel, n_row, n_col, row_tiles, col_til...]
    unnamed x4 -> x22, local copies, waits for them, and re-layouts: 5.81 us -> 9.23 us
    pallas_call x0 -> x1, Pallas kernels: none -> 1.99 us  [body(): pl.pallas_call(finish, out_shape=(jax.ShapeDtypeStruct((share, width), BF...]
where the time goes in v2:
time: 51.5 us; the launch traced here: 51.2 us
  Pallas kernels  40.6 us (79%)
  local copies, waits for them, and re-layouts  9.23 us (18%)
  between operations  1.31 us (3%)
    pallas_call x1, Pallas kernels, body(): pl.pallas_call(functools.partial(kernel, n_row, n_col, row_tiles, col_til...  38.7 us
    unnamed x22, local copies, waits for them, and re-layouts  9.23 us
    pallas_call x1, Pallas kernels, body(): pl.pallas_call(finish, out_shape=(jax.ShapeDtypeStruct((share, width), BF...  1.99 us

profile of v2, /device:TPU:0, one launch (start us, length us, event | category | flops | bytes accessed | tf_op | source)
XLA Modules:
  0.0 51.2 jit_solution(3126088376979592331)
XLA Ops:
  1.3 0.0 copy-start
  1.3 2.2 %copy-done = bf16[1,1,128,128,128]{4,3,2,1,0:T(8,128)(2,1)S(1)} copy-done((bf16[1,1,128,128,128]{4,3,2,1,0:T(8,128)(2,1)S(1)}, bf16[1,1,128,128,128]{4,3,2,1,0:T(8,128)(2,1)}, u32[]{:S(2)}) %copy-start) | copy-done | bytes 4194328
  3.5 0.0 copy-start.1
  3.5 0.9 %copy-done.1 = bf16[256,256]{1,0:T(8,128)(2,1)S(1)} copy-done((bf16[256,256]{1,0:T(8,128)(2,1)S(1)}, bf16[256,256]{1,0:T(8,128)(2,1)}, u32[]{:S(2)}) %copy-start.1) | copy-done | bytes 131096
  4.4 0.0 copy-start.3
  4.4 0.8 %copy-done.3 = bf16[128,256]{1,0:T(8,128)(2,1)S(1)} copy-done((bf16[128,256]{1,0:T(8,128)(2,1)S(1)}, bf16[128,256]{1,0:T(8,128)(2,1)}, u32[]{:S(2)}) %copy-start.3) | copy-done | bytes 65560
  5.2 0.0 copy-start.4
  5.2 0.8 %copy-done.4 = bf16[128,256]{1,0:T(8,128)(2,1)S(1)} copy-done((bf16[128,256]{1,0:T(8,128)(2,1)S(1)}, bf16[128,256]{1,0:T(8,128)(2,1)}, u32[]{:S(2)}) %copy-start.4) | copy-done | bytes 65560
  6.1 0.0 copy-start.8
  6.1 0.7 %copy-done.8 = f32[256]{0:T(256)S(1)} copy-done((f32[256]{0:T(256)S(1)}, f32[256]{0:T(256)}, u32[]{:S(2)}) %copy-start.8) | copy-done | bytes 1048
  6.7 0.0 copy-start.9
  6.7 0.7 %copy-done.9 = s32[1,1,128]{2,1,0:T(1,128)S(1)} copy-done((s32[1,1,128]{2,1,0:T(1,128)S(1)}, s32[1,1,128]{2,1,0:T(1,128)}, u32[]{:S(2)}) %copy-start.9) | copy-done | bytes 536
  7.4 0.0 copy-start.10
  7.4 0.7 %copy-done.10 = s32[1,1,128]{2,1,0:T(1,128)S(1)} copy-done((s32[1,1,128]{2,1,0:T(1,128)S(1)}, s32[1,1,128]{2,1,0:T(1,128)}, u32[]{:S(2)}) %copy-start.10) | copy-done | bytes 536
  8.0 38.7 %shard_map.111 = (bf16[128,256]{1,0:T(8,128)(2,1)S(1)}, bf16[128,256]{1,0:T(8,128)(2,1)S(1)}, bf16[8,32,256]{2,1,0:T(8,128)(2,1)S(1)}, f32[4,8,256]{2,1,0:T(8,128)S(1)}) custom-call(bf16[128,256]{1,0:T(8,128)(2,1)S(1)} %copy-done.3, bf16[256,256]{1,0:T(8,128)(2,1)S(1)} %copy-done.1, f32[1,256]{1,0:T(1,128)S(1)} %bitcast.6, bf16[128,256]{1,0:T(8,128)(2,1)S(1)} %copy-done.4, ...), custom_call_target="tpu_custom_call" | custom-call | flops 536870912 | bytes 4194304 | tf_op jit(solution)/shard_map/pallas_call | solution.py:343
  46.7 0.0 copy-start.2
  46.7 0.6 %copy-done.2 = bf16[8,32,256]{2,1,0:T(8,128)(2,1)} copy-done((bf16[8,32,256]{2,1,0:T(8,128)(2,1)}, bf16[8,32,256]{2,1,0:T(8,128)(2,1)S(1)}, u32[]{:S(2)}) %copy-start.2) | copy-done | bytes 131096
  47.4 0.0 copy-start.5
  47.4 0.6 %copy-done.5 = bf16[128,256]{1,0:T(8,128)(2,1)} copy-done((bf16[128,256]{1,0:T(8,128)(2,1)}, bf16[128,256]{1,0:T(8,128)(2,1)S(1)}, u32[]{:S(2)}) %copy-start.5) | copy-done | bytes 65560
  48.0 0.0 copy-start.6
  48.0 0.6 %copy-done.6 = bf16[128,256]{1,0:T(8,128)(2,1)} copy-done((bf16[128,256]{1,0:T(8,128)(2,1)}, bf16[128,256]{1,0:T(8,128)(2,1)S(1)}, u32[]{:S(2)}) %copy-start.6) | copy-done | bytes 65560
  48.6 0.0 copy-start.7
  48.6 0.6 %copy-done.7 = f32[4,8,256]{2,1,0:T(8,128)} copy-done((f32[4,8,256]{2,1,0:T(8,128)}, f32[4,8,256]{2,1,0:T(8,128)S(1)}, u32[]{:S(2)}) %copy-start.7) | copy-done | bytes 32792
  49.2 2.0 %shard_map.112 = (bf16[128,256]{1,0:T(8,128)(2,1)}, bf16[128,256]{1,0:T(8,128)(2,1)}, f32[256,256]{1,0:T(8,128)}, f32[1,256]{1,0:T(1,128)}) custom-call(bf16[128,256]{1,0:T(8,128)(2,1)} %copy-done.5, bf16[128,256]{1,0:T(8,128)(2,1)} %copy-done.6, bf16[8,32,256]{2,1,0:T(8,128)(2,1)} %copy-done.2, f32[4,8,256]{2,1,0:T(8,128)} %copy-done.7, ...), custom_call_target="tpu_custom_call" | custom-call | tf_op jit(solution)/shard_map/pallas_call | solution.py:367
Async XLA Ops:
  1.3 2.2 %copy-start = (bf16[1,1,128,128,128]{4,3,2,1,0:T(8,128)(2,1)S(1)}, bf16[1,1,128,128,128]{4,3,2,1,0:T(8,128)(2,1)}, u32[]{:S(2)}) copy-start(bf16[1,1,128,128,128]{4,3,2,1,0:T(8,128)(2,1)} %param.15) | copy-start | bytes 12582916
  3.5 0.9 %copy-start.1 = (bf16[256,256]{1,0:T(8,128)(2,1)S(1)}, bf16[256,256]{1,0:T(8,128)(2,1)}, u32[]{:S(2)}) copy-start(bf16[256,256]{1,0:T(8,128)(2,1)} %weight_ref.3) | copy-start | bytes 393220
  4.4 0.8 %copy-start.3 = (bf16[128,256]{1,0:T(8,128)(2,1)S(1)}, bf16[128,256]{1,0:T(8,128)(2,1)}, u32[]{:S(2)}) copy-start(bf16[128,256]{1,0:T(8,128)(2,1)} %feat_ref.1) | copy-start | bytes 196612
  5.2 0.8 %copy-start.4 = (bf16[128,256]{1,0:T(8,128)(2,1)S(1)}, bf16[128,256]{1,0:T(8,128)(2,1)}, u32[]{:S(2)}) copy-start(bf16[128,256]{1,0:T(8,128)(2,1)} %gout_ref.1) | copy-start | bytes 196612
  6.1 0.7 %copy-start.8 = (f32[256]{0:T(256)S(1)}, f32[256]{0:T(256)}, u32[]{:S(2)}) copy-start(f32[256]{0:T(256)} %param.10) | copy-start | bytes 3076
  6.7 0.7 %copy-start.9 = (s32[1,1,128]{2,1,0:T(1,128)S(1)}, s32[1,1,128]{2,1,0:T(1,128)}, u32[]{:S(2)}) copy-start(s32[1,1,128]{2,1,0:T(1,128)} %param.12) | copy-start | bytes 1540
  7.4 0.7 %copy-start.10 = (s32[1,1,128]{2,1,0:T(1,128)S(1)}, s32[1,1,128]{2,1,0:T(1,128)}, u32[]{:S(2)}) copy-start(s32[1,1,128]{2,1,0:T(1,128)} %param.13) | copy-start | bytes 1540
  46.7 0.7 %copy-start.2 = (bf16[8,32,256]{2,1,0:T(8,128)(2,1)}, bf16[8,32,256]{2,1,0:T(8,128)(2,1)S(1)}, u32[]{:S(2)}) copy-start(bf16[8,32,256]{2,1,0:T(8,128)(2,1)S(1)} %get-tuple-element.14.gwp_ref) | copy-start | bytes 393220
  47.4 0.6 %copy-start.5 = (bf16[128,256]{1,0:T(8,128)(2,1)}, bf16[128,256]{1,0:T(8,128)(2,1)S(1)}, u32[]{:S(2)}) copy-start(bf16[128,256]{1,0:T(8,128)(2,1)S(1)} %get-tuple-element.12.part_ref) | copy-start | bytes 196612
  48.0 0.6 %copy-start.6 = (bf16[128,256]{1,0:T(8,128)(2,1)}, bf16[128,256]{1,0:T(8,128)(2,1)S(1)}, u32[]{:S(2)}) copy-start(bf16[128,256]{1,0:T(8,128)(2,1)S(1)} %get-tuple-element.13.gmix_ref) | copy-start | bytes 196612
  48.6 0.6 %copy-start.7 = (f32[4,8,256]{2,1,0:T(8,128)}, f32[4,8,256]{2,1,0:T(8,128)S(1)}, u32[]{:S(2)}) copy-start(f32[4,8,256]{2,1,0:T(8,128)S(1)} %get-tuple-element.15.gbp_ref) | copy-start | bytes 98308

commit v3 on v2

--- a/solution.py
+++ b/solution.py
@@ -1,5 +1,4 @@
 import functools
-import math
 
 import jax
 import jax.numpy as jnp
@@ -10,6 +9,7 @@
 
 MESH = pl.DeviceIdType.MESH
 CHUNKS = 4
+VMEM_BYTES = 60 * 2**20
 F32 = jnp.float32
 BF16 = jnp.bfloat16
 
@@ -24,11 +24,12 @@
 
 def kernel(
     n_row, n_col, row_tiles, col_tiles,
-    feat_ref, weight_ref, bias_ref, gout_ref, rows_ref, cols_ref, count_ref, values_ref,
-    out_ref, gmix_ref, gw_ref, gb_ref,
+    feat_ref, weight_hbm, bias_hbm, gout_hbm, rows_hbm, cols_hbm, count_ref, values_ref,
+    out_hbm, gmix_ref, gw_hbm, gb_hbm,
+    weight_ref, bias_ref, gout_ref, rows_ref, cols_ref, out_ref,
     vals, seq, dense, dense_t, feat_all, pair_send, pair_recv, part_send, part_recv, grad_all,
     back_send, back_recv, gw_send, gw_recv, gwz_recv, gw_all, gb_recv, idx_v, idx_s,
-    val_sem, idx_sem, f_send, f_recv, p_send, p_recv, q_send, q_recv, g_send, g_recv,
+    val_sem, idx_sem, in_sem, out_sem, f_send, f_recv, p_send, p_recv, q_send, q_recv, g_send, g_recv,
     h_send, h_recv, b_send, b_recv,
     w_send, w_recv, z_send, z_recv, a_send, a_recv, s_send, s_recv,
 ):
@@ -65,8 +66,18 @@
         return pltpu.make_async_copy(
             values_ref.at[pl.ds(q * per, per)], vals.at[pl.ds(q * per, per)], val_sem.at[q])
 
+    bring = [
+        pltpu.make_async_copy(src, dst, in_sem.at[i])
+        for i, (src, dst) in enumerate((
+            (rows_hbm, rows_ref), (cols_hbm, cols_ref), (feat_ref, feat_all.at[my_r]),
+            (weight_hbm, weight_ref), (bias_hbm, bias_ref), (gout_hbm, gout_ref)))
+    ]
+    bring[0].start()
+    bring[1].start()
     for q in range(CHUNKS):
         fetch(q).start()
+    for copy in bring[2:]:
+        copy.start()
 
     barrier = pltpu.get_barrier_semaphore()
     for d in range(1, n_row):
@@ -78,6 +89,8 @@
     lane = lax.broadcasted_iota(jnp.int32, (slots, slots), 1)
     sub = lax.broadcasted_iota(jnp.int32, (slots, slots), 0)
     live = lane < count_ref[0, 0]
+    bring[0].wait()
+    bring[1].wait()
     key = jnp.where(
         live, jnp.broadcast_to(rows_ref[...] * col_tiles + cols_ref[...], (slots, slots)), tiles)
     key_t = key.T
@@ -99,7 +112,6 @@
 
     for d in range(1, n_row):
         feat_copy(d).start()
-    feat_all[my_r] = feat_ref[...]
 
     idx_copy.wait()
     for q in range(CHUNKS):
@@ -134,6 +146,8 @@
 
     lax.fori_loop(0, row_tiles, place, 0)
 
+    for copy in bring[2:]:
+        copy.wait()
     for d in range(1, n_row):
         feat_copy(d).wait_recv()
 
@@ -201,6 +215,8 @@
         grad_copy(d).start()
     hand_copy(0).start()
     out_ref[...] = jnp.where(pre > 0, pre, low - 1.0).astype(BF16)
+    out_copy = pltpu.make_async_copy(out_ref, out_hbm, out_sem.at[0])
+    out_copy.start()
 
     def gw_copy(d):
         return to_col(gw_send.at[col_peer(d)], gw_recv.at[d], w_send, w_recv, d, col_peer(d))
@@ -273,7 +289,8 @@
 
     for d in range(1, n_row):
         gb_copy(d).wait_recv()
-    gb_ref[...] = gb_recv[...]
+    gb_copy_out = pltpu.make_async_copy(gb_recv, gb_hbm, out_sem.at[1])
+    gb_copy_out.start()
 
     for d in range(1, n_row):
         feat_copy(d).wait_send()
@@ -287,11 +304,15 @@
         part_copy(d).wait_send()
         grad_copy(d).wait_send()
     for d in range(1, n_col):
+        all_copy(d).wait_recv()
+    gw_copy_out = pltpu.make_async_copy(gw_all, gw_hbm, out_sem.at[2])
+    gw_copy_out.start()
+    for d in range(1, n_col):
         gw_copy(d).wait_send()
-        all_copy(d).wait_recv()
-    gw_ref[...] = gw_all[...]
-    for d in range(1, n_col):
         all_copy(d).wait_send()
+    out_copy.wait()
+    gb_copy_out.wait()
+    gw_copy_out.wait()
 
 
 def finish(part_ref, gmix_ref, gwp_ref, gbp_ref, weight_ref, out_ref, gfeat_ref, gw_ref, gb_ref):
@@ -317,9 +338,16 @@
     index_rows = -(-(2 + -(-(row_tiles * col_tiles) // slots)) // 8) * 8
     vmem = pl.BlockSpec(memory_space=pltpu.VMEM)
     smem = pl.BlockSpec(memory_space=pltpu.SMEM)
+    anywhere = pl.BlockSpec(memory_space=pl.ANY)
     dma = pltpu.SemaphoreType.DMA
     row_sem, col_sem, chip_sem = dma((n_row,)), dma((n_col,)), dma((n_col // 2,))
     buffers = [
+        ((width, width), BF16),
+        ((1, width), F32),
+        ((share, width), BF16),
+        ((1, slots), jnp.int32),
+        ((1, slots), jnp.int32),
+        ((share, width), BF16),
         ((slots, side, side), BF16),
         ((slots, side, side), BF16),
         ((row_tiles * side, col_tiles * side), BF16),
@@ -339,7 +367,6 @@
         ((n_row, 8, width), F32),
         ((index_rows, slots), jnp.int32),
     ]
-    held = sum(math.prod(shape) * jnp.dtype(kind).itemsize for shape, kind in buffers)
     out, gmix, gw, gb = pl.pallas_call(
         functools.partial(kernel, n_row, n_col, row_tiles, col_tiles),
         out_shape=(
@@ -348,18 +375,18 @@
             jax.ShapeDtypeStruct((n_col, chunk, width), gw_type),
             jax.ShapeDtypeStruct((n_row, 8, width), F32),
         ),
-        in_specs=[vmem] * 6 + [smem, pl.BlockSpec(memory_space=pltpu.HBM)],
-        out_specs=(vmem, vmem, vmem, vmem),
+        in_specs=[anywhere] * 6 + [smem, anywhere],
+        out_specs=(anywhere, vmem, anywhere, anywhere),
         scratch_shapes=[pltpu.VMEM(shape, kind) for shape, kind in buffers] + [
             pltpu.SMEM((index_rows, slots), jnp.int32),
-            dma((CHUNKS,)), dma(()),
+            dma((CHUNKS,)), dma(()), dma((6,)), dma((3,)),
             row_sem, row_sem, chip_sem, chip_sem, chip_sem, chip_sem, chip_sem, chip_sem,
             chip_sem, chip_sem, row_sem, row_sem,
             col_sem, col_sem, row_sem, row_sem, col_sem, col_sem, row_sem, row_sem,
         ],
         compiler_params=pltpu.CompilerParams(
             collective_id=0, has_side_effects=True,
-            vmem_limit_bytes=min(60 * 2**20, held + 12 * 2**20)),
+            vmem_limit_bytes=VMEM_BYTES),
         cost_estimate=pl.CostEstimate(
             flops=4 * row_tiles * col_tiles * side * side * width,
             bytes_accessed=2 * slots * side * side, transcendentals=share * width),
@@ -374,6 +401,7 @@
         ),
         in_specs=[vmem] * 5,
         out_specs=(vmem, vmem, vmem, vmem),
+        compiler_params=pltpu.CompilerParams(vmem_limit_bytes=VMEM_BYTES),
     )(out, gmix, gw, gb, weight)
     return out, gfeat, gw, gb[0]
 

time: 51.5 us -> 43.4 us (0.84)
  local copies, waits for them, and re-layouts: 9.23 us -> 0 us
  Pallas kernels: 40.6 us -> 41.9 us
    unnamed x22 -> x0, local copies, waits for them, and re-layouts: 9.23 us -> none
    pallas_call x1, Pallas kernels: 38.7 us -> 39.9 us  [body(): pl.pallas_call(functools.partial(kernel, n_row, n_col, row_tiles, col_til...]
where the time goes in v3:
time: 43.4 us; the launch traced here: 43.2 us
  Pallas kernels  41.9 us (97%)
  between operations  1.29 us (3%)
    pallas_call x1, Pallas kernels, body(): pl.pallas_call(functools.partial(kernel, n_row, n_col, row_tiles, col_til...  39.9 us
    pallas_call x1, Pallas kernels, body(): pl.pallas_call(finish, out_shape=(jax.ShapeDtypeStruct((share, width), BF...  2 us

profile of v3, /device:TPU:0, one launch (start us, length us, event | category | flops | bytes accessed | tf_op | source)
XLA Modules:
  0.0 43.2 jit_solution(2908161403462791464)
XLA Ops:
  1.3 39.9 %shard_map.111 = (bf16[128,256]{1,0:T(8,128)(2,1)}, bf16[128,256]{1,0:T(8,128)(2,1)}, bf16[8,32,256]{2,1,0:T(8,128)(2,1)}, f32[4,8,256]{2,1,0:T(8,128)}) custom-call(bf16[128,256]{1,0:T(8,128)(2,1)} %feat_ref.1, bf16[256,256]{1,0:T(8,128)(2,1)} %weight_ref.1, f32[1,256]{1,0:T(1,128)} %bitcast.6, bf16[128,256]{1,0:T(8,128)(2,1)} %gout_hbm.1, ...), custom_call_target="tpu_custom_call" | custom-call | flops 536870912 | bytes 4194304 | tf_op jit(solution)/shard_map/pallas_call | solution.py:370
  41.2 2.0 %shard_map.112 = (bf16[128,256]{1,0:T(8,128)(2,1)}, bf16[128,256]{1,0:T(8,128)(2,1)}, f32[256,256]{1,0:T(8,128)}, f32[1,256]{1,0:T(1,128)}) custom-call(bf16[128,256]{1,0:T(8,128)(2,1)} %get-tuple-element.12.part_ref, bf16[128,256]{1,0:T(8,128)(2,1)} %get-tuple-element.13.gmix_ref, bf16[8,32,256]{2,1,0:T(8,128)(2,1)} %get-tuple-element.14.gwp_ref, ...), custom_call_target="tpu_custom_call" | custom-call | tf_op jit(solution)/shard_map/pallas_call | solution.py:394

commit v4 on v3

--- a/solution.py
+++ b/solution.py
@@ -28,6 +28,7 @@
     out_hbm, gmix_ref, gw_hbm, gb_hbm,
     weight_ref, bias_ref, gout_ref, rows_ref, cols_ref, out_ref,
     vals, seq, dense, dense_t, feat_all, pair_send, pair_recv, part_send, part_recv, grad_all,
+    own_sum, back_sum,
     back_send, back_recv, gw_send, gw_recv, gwz_recv, gw_all, gb_recv, idx_v, idx_s,
     val_sem, idx_sem, in_sem, out_sem, f_send, f_recv, p_send, p_recv, q_send, q_recv, g_send, g_recv,
     h_send, h_recv, b_send, b_recv,
@@ -84,6 +85,14 @@
         pl.semaphore_signal(barrier, inc=1, device_id=(row_peer(d), my_c), device_id_type=MESH)
     for d in range(1, n_col):
         pl.semaphore_signal(barrier, inc=1, device_id=(my_r, col_peer(d)), device_id_type=MESH)
+
+    pl.semaphore_wait(barrier, n_row + n_col - 2)
+
+    def feat_copy(d):
+        return to_row(feat_ref, feat_all.at[my_r], f_send, f_recv, d)
+
+    for d in range(1, n_row):
+        feat_copy(d).start()
 
     tiles = row_tiles * col_tiles
     lane = lax.broadcasted_iota(jnp.int32, (slots, slots), 1)
@@ -105,13 +114,6 @@
     idx_copy = pltpu.make_async_copy(idx_v, idx_s, idx_sem)
     idx_copy.start()
 
-    pl.semaphore_wait(barrier, n_row + n_col - 2)
-
-    def feat_copy(d):
-        return to_row(feat_ref, feat_all.at[my_r], f_send, f_recv, d)
-
-    for d in range(1, n_row):
-        feat_copy(d).start()
 
     idx_copy.wait()
     for q in range(CHUNKS):
@@ -151,34 +153,47 @@
     for d in range(1, n_row):
         feat_copy(d).wait_recv()
 
-    def aggregate(block):
+    half = n_chip * share
+
+    def group(n, step):
+        size = 4 if n % 4 == 0 else 1
+        each(n // size, lambda g: step(g * size * share, size * share))
+
+    def rows_at(start, count):
+        return pl.ds(pl.multiple_of(start, share), count)
+
+    def aggregate(start, count):
         return jnp.dot(
-            dense[pl.ds(pl.multiple_of(block * share, share), share), :],
-            feat_all[...].reshape(n_row * share, width), preferred_element_type=F32)
+            dense[rows_at(start, count), :], feat_all[...].reshape(n_row * share, width),
+            preferred_element_type=F32)
+
+    def chip_rows(d):
+        return rows_at(lax.rem(chip + d, n_chip) * share, share)
 
     def pair_copy(d):
-        return to_col(pair_send.at[d], pair_recv.at[d], p_send, p_recv, d, sibling)
+        return to_col(
+            pair_send.at[chip_rows(d), :], pair_recv.at[d], p_send, p_recv, d, sibling)
 
     def part_copy(d):
         return to_col(part_send.at[d], part_recv.at[d], q_send, q_recv, d, chip_peer(d))
 
-    def pair_step(i):
-        d = lax.rem(i + 1, n_chip)
-        pair_send[d] = aggregate((1 - core) * n_chip + lax.rem(chip + d, n_chip)).astype(BF16)
-        pair_copy(d).start()
-
-    def part_step(i):
-        d = i + 1
-        mine = aggregate(core * n_chip + lax.rem(chip + d, n_chip))
+    def pair_step(start, count):
+        pair_send[rows_at(start, count), :] = (
+            aggregate((1 - core) * half + start, count).astype(BF16))
+
+    def own_step(start, count):
+        own_sum[rows_at(start, count), :] = aggregate(core * half + start, count)
+
+    group(n_chip, pair_step)
+    for d in range(n_chip):
+        pair_copy((d + 1) % n_chip).start()
+    group(n_chip, own_step)
+    for d in range(1, n_chip):
         pair_copy(d).wait_recv()
-        part_send[d] = (mine + pair_recv[d].astype(F32)).astype(BF16)
+        part_send[d] = (own_sum[chip_rows(d), :] + pair_recv[d].astype(F32)).astype(BF16)
         part_copy(d).start()
-
-    each(n_chip, pair_step)
-    each(n_chip - 1, part_step)
-    gathered = aggregate(core * n_chip + chip)
     pair_copy(0).wait_recv()
-    gathered = gathered + pair_recv[0].astype(F32)
+    gathered = own_sum[chip_rows(0), :] + pair_recv[0].astype(F32)
 
     def turn(r, _):
         for c in range(col_tiles):
@@ -229,35 +244,44 @@
     for d in range(1, n_chip):
         grad_copy(d).wait_recv()
         hand_copy(d).start()
+    def back_copy(d):
+        return to_row(back_send.at[d], back_recv.at[d], b_send, b_recv, d)
+
+    def half_product(start, count, side_core):
+        at = pl.ds(pl.multiple_of(side_core * half, share), half)
+        return jnp.dot(
+            dense_t[rows_at(start, count), at], grad_all[at, :], preferred_element_type=F32)
+
+    def first_step(start, count):
+        back_sum[rows_at(start, count), :] = half_product(start, count, core)
+
+    def backward(i):
+        return back_sum[rows_at(i * share, share), :] + half_product(i * share, share, 1 - core)
+
+    group(n_row, first_step)
     for d in range(n_chip):
         hand_copy(d).wait_recv()
-
-    def back_copy(d):
-        return to_row(back_send.at[d], back_recv.at[d], b_send, b_recv, d)
-
-    def backward(i):
-        return jnp.dot(
-            dense_t[pl.ds(pl.multiple_of(i * share, share), share), :], grad_all[...],
-            preferred_element_type=F32)
+    back_send[1] = backward(row_peer(1)).astype(BF16)
+
+    gw_sum = gw_send[my_c].astype(F32)
+    for d in range(1, n_col):
+        gw_copy(d).wait_recv()
+        gw_sum = gw_sum + gw_recv[d].astype(F32)
+
+    def gwz_copy(d):
+        return to_row(gwz_recv.at[my_r], gwz_recv.at[my_r], z_send, z_recv, d)
+
+    gwz_recv[my_r] = gw_sum.astype(gw_send.dtype)
+    for d in range(1, n_row):
+        gwz_copy(d).start()
+    back_copy(1).start()
 
     def backward_send(i):
-        d = i + 1
+        d = i + 2
         back_send[d] = backward(row_peer(d)).astype(BF16)
         back_copy(d).start()
 
-    each(n_row - 1, backward_send)
-
-    gw_sum = gw_send[my_c].astype(F32)
-    for d in range(1, n_col):
-        gw_copy(d).wait_recv()
-        gw_sum = gw_sum + gw_recv[d].astype(F32)
-
-    def gwz_copy(d):
-        return to_row(gwz_recv.at[my_r], gwz_recv.at[my_r], z_send, z_recv, d)
-
-    gwz_recv[my_r] = gw_sum.astype(gw_send.dtype)
-    for d in range(1, n_row):
-        gwz_copy(d).start()
+    each(n_row - 2, backward_send)
 
     def gb_copy(d):
         return to_row(gb_recv.at[my_r], gb_recv.at[my_r], s_send, s_recv, d)
@@ -353,11 +377,13 @@
         ((row_tiles * side, col_tiles * side), BF16),
         ((col_tiles * side, row_tiles * side), BF16),
         ((n_row, share, width), BF16),
-        ((n_col // 2, share, width), BF16),
+        ((n_col // 2 * share, width), BF16),
         ((n_col // 2, share, width), BF16),
         ((n_col // 2, share, width), BF16),
         ((n_col // 2, share, width), BF16),
         ((n_col * share, width), BF16),
+        ((n_col // 2 * share, width), F32),
+        ((n_row * share, width), F32),
         ((n_row, share, width), BF16),
         ((n_row, share, width), BF16),
         ((n_col, chunk, width), gw_type),

time: 43.4 us -> 41.1 us (0.947)
  Pallas kernels: 41.9 us -> 39.6 us
    pallas_call x1, Pallas kernels: 39.9 us -> 37.6 us  [body(): pl.pallas_call(functools.partial(kernel, n_row, n_col, row_tiles, col_til...]
where the time goes in v4:
time: 41.1 us; the launch traced here: 40.9 us
  Pallas kernels  39.6 us (96%)
  between operations  1.29 us (3%)
    pallas_call x1, Pallas kernels, body(): pl.pallas_call(functools.partial(kernel, n_row, n_col, row_tiles, col_til...  37.6 us
    pallas_call x1, Pallas kernels, body(): pl.pallas_call(finish, out_shape=(jax.ShapeDtypeStruct((share, width), BF...  2 us

profile of v4, /device:TPU:0, one launch (start us, length us, event | category | flops | bytes accessed | tf_op | source)
XLA Modules:
  0.0 40.9 jit_solution(5009318528869800641)
XLA Ops:
  1.3 37.6 %shard_map.111 = (bf16[128,256]{1,0:T(8,128)(2,1)}, bf16[128,256]{1,0:T(8,128)(2,1)}, bf16[8,32,256]{2,1,0:T(8,128)(2,1)}, f32[4,8,256]{2,1,0:T(8,128)}) custom-call(bf16[128,256]{1,0:T(8,128)(2,1)} %feat_ref.1, bf16[256,256]{1,0:T(8,128)(2,1)} %weight_ref.1, f32[1,256]{1,0:T(1,128)} %bitcast.6, bf16[128,256]{1,0:T(8,128)(2,1)} %gout_hbm.1, ...), custom_call_target="tpu_custom_call" | custom-call | flops 536870912 | bytes 4194304 | tf_op jit(solution)/shard_map/pallas_call | solution.py:396
  38.9 2.0 %shard_map.112 = (bf16[128,256]{1,0:T(8,128)(2,1)}, bf16[128,256]{1,0:T(8,128)(2,1)}, f32[256,256]{1,0:T(8,128)}, f32[1,256]{1,0:T(1,128)}) custom-call(bf16[128,256]{1,0:T(8,128)(2,1)} %get-tuple-element.12.part_ref, bf16[128,256]{1,0:T(8,128)(2,1)} %get-tuple-element.13.gmix_ref, bf16[8,32,256]{2,1,0:T(8,128)(2,1)} %get-tuple-element.14.gwp_ref, ...), custom_call_target="tpu_custom_call" | custom-call | tf_op jit(solution)/shard_map/pallas_call | solution.py:420

commit v5 on v4

--- a/solution.py
+++ b/solution.py
@@ -9,6 +9,7 @@
 
 MESH = pl.DeviceIdType.MESH
 CHUNKS = 4
+PARTS = 2
 VMEM_BYTES = 60 * 2**20
 F32 = jnp.float32
 BF16 = jnp.bfloat16
@@ -43,6 +44,10 @@
     share, width = feat_ref.shape
     per = slots // CHUNKS
     chunk = width // n_col
+    part = width // PARTS
+
+    def lanes(h):
+        return slice(h * part, (h + 1) * part)
 
     def row_peer(d):
         return lax.rem(my_r + d, n_row)
@@ -53,14 +58,14 @@
     def chip_peer(d):
         return 2 * lax.rem(chip + d, n_chip) + core
 
-    def to_row(src, dst, send, recv, d):
+    def to_row(src, dst, send, recv, d, h=0):
         return pltpu.make_async_remote_copy(
-            src_ref=src, dst_ref=dst, send_sem=send.at[d], recv_sem=recv.at[d],
+            src_ref=src, dst_ref=dst, send_sem=send.at[h * n_row + d], recv_sem=recv.at[h * n_row + d],
             device_id=(row_peer(d), my_c), device_id_type=MESH)
 
-    def to_col(src, dst, send, recv, d, peer):
+    def to_col(src, dst, send, recv, d, peer, h=0):
         return pltpu.make_async_remote_copy(
-            src_ref=src, dst_ref=dst, send_sem=send.at[d], recv_sem=recv.at[d],
+            src_ref=src, dst_ref=dst, send_sem=send.at[h * n_chip + d], recv_sem=recv.at[h * n_chip + d],
             device_id=(my_r, peer), device_id_type=MESH)
 
     def fetch(q):
@@ -70,8 +75,9 @@
     bring = [
         pltpu.make_async_copy(src, dst, in_sem.at[i])
         for i, (src, dst) in enumerate((
-            (rows_hbm, rows_ref), (cols_hbm, cols_ref), (feat_ref, feat_all.at[my_r]),
-            (weight_hbm, weight_ref), (bias_hbm, bias_ref), (gout_hbm, gout_ref)))
+            (rows_hbm, rows_ref), (cols_hbm, cols_ref), (weight_hbm, weight_ref),
+            (bias_hbm, bias_ref), (gout_hbm, gout_ref),
+            *((feat_ref.at[:, lanes(h)], feat_all.at[h, my_r]) for h in range(PARTS))))
     ]
     bring[0].start()
     bring[1].start()
@@ -88,11 +94,12 @@
 
     pl.semaphore_wait(barrier, n_row + n_col - 2)
 
-    def feat_copy(d):
-        return to_row(feat_ref, feat_all.at[my_r], f_send, f_recv, d)
-
-    for d in range(1, n_row):
-        feat_copy(d).start()
+    def feat_copy(d, h):
+        return to_row(feat_ref.at[:, lanes(h)], feat_all.at[h, my_r], f_send, f_recv, d, h)
+
+    for h in range(PARTS):
+        for d in range(1, n_row):
+            feat_copy(d, h).start()
 
     tiles = row_tiles * col_tiles
     lane = lax.broadcasted_iota(jnp.int32, (slots, slots), 1)
@@ -150,9 +157,6 @@
 
     for copy in bring[2:]:
         copy.wait()
-    for d in range(1, n_row):
-        feat_copy(d).wait_recv()
-
     half = n_chip * share
 
     def group(n, step):
@@ -162,38 +166,42 @@
     def rows_at(start, count):
         return pl.ds(pl.multiple_of(start, share), count)
 
-    def aggregate(start, count):
+    def aggregate(start, count, h):
         return jnp.dot(
-            dense[rows_at(start, count), :], feat_all[...].reshape(n_row * share, width),
+            dense[rows_at(start, count), :], feat_all[h].reshape(n_row * share, part),
             preferred_element_type=F32)
 
     def chip_rows(d):
         return rows_at(lax.rem(chip + d, n_chip) * share, share)
 
-    def pair_copy(d):
+    def pair_copy(d, h):
         return to_col(
-            pair_send.at[chip_rows(d), :], pair_recv.at[d], p_send, p_recv, d, sibling)
-
-    def part_copy(d):
-        return to_col(part_send.at[d], part_recv.at[d], q_send, q_recv, d, chip_peer(d))
-
-    def pair_step(start, count):
-        pair_send[rows_at(start, count), :] = (
-            aggregate((1 - core) * half + start, count).astype(BF16))
-
-    def own_step(start, count):
-        own_sum[rows_at(start, count), :] = aggregate(core * half + start, count)
-
-    group(n_chip, pair_step)
-    for d in range(n_chip):
-        pair_copy((d + 1) % n_chip).start()
-    group(n_chip, own_step)
-    for d in range(1, n_chip):
-        pair_copy(d).wait_recv()
-        part_send[d] = (own_sum[chip_rows(d), :] + pair_recv[d].astype(F32)).astype(BF16)
-        part_copy(d).start()
-    pair_copy(0).wait_recv()
-    gathered = own_sum[chip_rows(0), :] + pair_recv[0].astype(F32)
+            pair_send.at[h, chip_rows(d), :], pair_recv.at[h, d], p_send, p_recv, d, sibling, h)
+
+    def part_copy(d, h):
+        return to_col(
+            part_send.at[h, d], part_recv.at[h, d], q_send, q_recv, d, chip_peer(d), h)
+
+    for h in range(PARTS):
+        def pair_step(start, count):
+            pair_send[h, rows_at(start, count), :] = (
+                aggregate((1 - core) * half + start, count, h).astype(BF16))
+
+        def own_step(start, count):
+            own_sum[h, rows_at(start, count), :] = aggregate(core * half + start, count, h)
+
+        for d in range(1, n_row):
+            feat_copy(d, h).wait_recv()
+        group(n_chip, pair_step)
+        for d in range(n_chip):
+            pair_copy((d + 1) % n_chip, h).start()
+        group(n_chip, own_step)
+        for d in range(1, n_chip):
+            pair_copy(d, h).wait_recv()
+            part_send[h, d] = (
+                own_sum[h, chip_rows(d), :] + pair_recv[h, d].astype(F32)).astype(BF16)
+            part_copy(d, h).start()
+        pair_copy(0, h).wait_recv()
 
     def turn(r, _):
         for c in range(col_tiles):
@@ -204,31 +212,39 @@
 
     lax.fori_loop(0, row_tiles, turn, 0)
 
-    for d in range(1, n_chip):
-        part_copy(d).wait_recv()
-        gathered = gathered + part_recv[d].astype(F32)
+    sums = []
+    for h in range(PARTS):
+        total = own_sum[h, chip_rows(0), :] + pair_recv[h, 0].astype(F32)
+        for d in range(1, n_chip):
+            part_copy(d, h).wait_recv()
+            total = total + part_recv[h, d].astype(F32)
+        sums.append(total)
+    gathered = jnp.concatenate(sums, axis=1)
 
     pre = jnp.dot(
         gathered.astype(BF16), weight_ref[...], preferred_element_type=F32) + bias_ref[...]
     low = jnp.exp(jnp.minimum(pre, 0.0))
     grad = (gout_ref[...].astype(F32) * jnp.where(pre > 0, 1.0, low)).astype(BF16)
 
-    def rows_of(block):
-        return grad_all.at[pl.ds(pl.multiple_of(block * share, share), share), :]
+    def rows_of(block, h):
+        return grad_all.at[h, rows_at(block * share, share), :]
 
     mine_at = core * n_chip + chip
-    grad_all[pl.ds(pl.multiple_of(mine_at * share, share), share), :] = grad
-
-    def grad_copy(d):
-        return to_col(rows_of(mine_at), rows_of(mine_at), g_send, g_recv, d, chip_peer(d))
-
-    def hand_copy(d):
+    for h in range(PARTS):
+        grad_all[h, rows_at(mine_at * share, share), :] = grad[:, lanes(h)]
+
+    def grad_copy(d, h):
+        return to_col(
+            rows_of(mine_at, h), rows_of(mine_at, h), g_send, g_recv, d, chip_peer(d), h)
+
+    def hand_copy(d, h):
         at = core * n_chip + lax.rem(chip + n_chip - d, n_chip)
-        return to_col(rows_of(at), rows_of(at), h_send, h_recv, d, sibling)
-
-    for d in range(1, n_chip):
-        grad_copy(d).start()
-    hand_copy(0).start()
+        return to_col(rows_of(at, h), rows_of(at, h), h_send, h_recv, d, sibling, h)
+
+    for h in range(PARTS):
+        for d in range(1, n_chip):
+            grad_copy(d, h).start()
+        hand_copy(0, h).start()
     out_ref[...] = jnp.where(pre > 0, pre, low - 1.0).astype(BF16)
     out_copy = pltpu.make_async_copy(out_ref, out_hbm, out_sem.at[0])
     out_copy.start()
@@ -241,57 +257,57 @@
     for d in range(1, n_col):
         gw_copy(d).start()
 
-    for d in range(1, n_chip):
-        grad_copy(d).wait_recv()
-        hand_copy(d).start()
-    def back_copy(d):
-        return to_row(back_send.at[d], back_recv.at[d], b_send, b_recv, d)
-
-    def half_product(start, count, side_core):
+    def back_copy(d, h):
+        return to_row(back_send.at[h, d], back_recv.at[h, d], b_send, b_recv, d, h)
+
+    def half_product(start, count, side_core, h):
         at = pl.ds(pl.multiple_of(side_core * half, share), half)
         return jnp.dot(
-            dense_t[rows_at(start, count), at], grad_all[at, :], preferred_element_type=F32)
-
-    def first_step(start, count):
-        back_sum[rows_at(start, count), :] = half_product(start, count, core)
-
-    def backward(i):
-        return back_sum[rows_at(i * share, share), :] + half_product(i * share, share, 1 - core)
-
-    group(n_row, first_step)
-    for d in range(n_chip):
-        hand_copy(d).wait_recv()
-    back_send[1] = backward(row_peer(1)).astype(BF16)
-
-    gw_sum = gw_send[my_c].astype(F32)
-    for d in range(1, n_col):
-        gw_copy(d).wait_recv()
-        gw_sum = gw_sum + gw_recv[d].astype(F32)
+            dense_t[rows_at(start, count), at], grad_all[h, at, :], preferred_element_type=F32)
+
+    def backward(i, h):
+        return (back_sum[h, rows_at(i * share, share), :]
+                + half_product(i * share, share, 1 - core, h))
 
     def gwz_copy(d):
         return to_row(gwz_recv.at[my_r], gwz_recv.at[my_r], z_send, z_recv, d)
 
-    gwz_recv[my_r] = gw_sum.astype(gw_send.dtype)
-    for d in range(1, n_row):
-        gwz_copy(d).start()
-    back_copy(1).start()
-
-    def backward_send(i):
-        d = i + 2
-        back_send[d] = backward(row_peer(d)).astype(BF16)
-        back_copy(d).start()
-
-    each(n_row - 2, backward_send)
+    for h in range(PARTS):
+        def first_step(start, count):
+            back_sum[h, rows_at(start, count), :] = half_product(start, count, core, h)
+
+        def backward_send(i):
+            d = i + 1
+            back_send[h, d] = backward(row_peer(d), h).astype(BF16)
+            back_copy(d, h).start()
+
+        for d in range(1, n_chip):
+            grad_copy(d, h).wait_recv()
+            hand_copy(d, h).start()
+        group(n_row, first_step)
+        for d in range(n_chip):
+            hand_copy(d, h).wait_recv()
+        each(n_row - 1, backward_send)
+        if h == 0:
+            gw_sum = gw_send[my_c].astype(F32)
+            for d in range(1, n_col):
+                gw_copy(d).wait_recv()
+                gw_sum = gw_sum + gw_recv[d].astype(F32)
+            gwz_recv[my_r] = gw_sum.astype(gw_send.dtype)
+            for d in range(1, n_row):
+                gwz_copy(d).start()
 
     def gb_copy(d):
         return to_row(gb_recv.at[my_r], gb_recv.at[my_r], s_send, s_recv, d)
 
     ones = jnp.ones((16, n_col * share), BF16)
-    gb_recv[my_r] = jnp.dot(ones, grad_all[...], preferred_element_type=F32)[:8]
+    for h in range(PARTS):
+        gb_recv[my_r, :, lanes(h)] = jnp.dot(
+            ones, grad_all[h], preferred_element_type=F32)[:8]
     for d in range(1, n_row):
         gb_copy(d).start()
 
-    total = backward(my_r)
+    totals = [backward(my_r, h) for h in range(PARTS)]
 
     for d in range(1, n_row):
         gwz_copy(d).wait_recv()
@@ -306,10 +322,12 @@
     for d in range(1, n_col):
         all_copy(d).start()
 
-    for d in range(1, n_row):
-        back_copy(d).wait_recv()
-        total = total + back_recv[d].astype(F32)
-    gmix_ref[...] = total.astype(BF16)
+    for h in range(PARTS):
+        total = totals[h]
+        for d in range(1, n_row):
+            back_copy(d, h).wait_recv()
+            total = total + back_recv[h, d].astype(F32)
+        gmix_ref[:, lanes(h)] = total.astype(BF16)
 
     for d in range(1, n_row):
         gb_copy(d).wait_recv()
@@ -317,16 +335,18 @@
     gb_copy_out.start()
 
     for d in range(1, n_row):
-        feat_copy(d).wait_send()
-        back_copy(d).wait_send()
         gwz_copy(d).wait_send()
         gb_copy(d).wait_send()
-    for d in range(n_chip):
-        pair_copy(d).wait_send()
-        hand_copy(d).wait_send()
-    for d in range(1, n_chip):
-        part_copy(d).wait_send()
-        grad_copy(d).wait_send()
+    for h in range(PARTS):
+        for d in range(1, n_row):
+            feat_copy(d, h).wait_send()
+            back_copy(d, h).wait_send()
+        for d in range(n_chip):
+            pair_copy(d, h).wait_send()
+            hand_copy(d, h).wait_send()
+        for d in range(1, n_chip):
+            part_copy(d, h).wait_send()
+            grad_copy(d, h).wait_send()
     for d in range(1, n_col):
         all_copy(d).wait_recv()
     gw_copy_out = pltpu.make_async_copy(gw_all, gw_hbm, out_sem.at[2])
@@ -364,7 +384,8 @@
     smem = pl.BlockSpec(memory_space=pltpu.SMEM)
     anywhere = pl.BlockSpec(memory_space=pl.ANY)
     dma = pltpu.SemaphoreType.DMA
-    row_sem, col_sem, chip_sem = dma((n_row,)), dma((n_col,)), dma((n_col // 2,))
+    part = width // PARTS
+    row_sem, col_sem, chip_sem = dma((PARTS * n_row,)), dma((n_col,)), dma((PARTS * (n_col // 2),))
     buffers = [
         ((width, width), BF16),
         ((1, width), F32),
@@ -376,16 +397,16 @@
         ((slots, side, side), BF16),
         ((row_tiles * side, col_tiles * side), BF16),
         ((col_tiles * side, row_tiles * side), BF16),
-        ((n_row, share, width), BF16),
-        ((n_col // 2 * share, width), BF16),
-        ((n_col // 2, share, width), BF16),
-        ((n_col // 2, share, width), BF16),
-        ((n_col // 2, share, width), BF16),
-        ((n_col * share, width), BF16),
-        ((n_col // 2 * share, width), F32),
-        ((n_row * share, width), F32),
-        ((n_row, share, width), BF16),
-        ((n_row, share, width), BF16),
+        ((PARTS, n_row, share, part), BF16),
+        ((PARTS, n_col // 2 * share, part), BF16),
+        ((PARTS, n_col // 2, share, part), BF16),
+        ((PARTS, n_col // 2, share, part), BF16),
+        ((PARTS, n_col // 2, share, part), BF16),
+        ((PARTS, n_col * share, part), BF16),
+        ((PARTS, n_col // 2 * share, part), F32),
+        ((PARTS, n_row * share, part), F32),
+        ((PARTS, n_row, share, part), BF16),
+        ((PARTS, n_row, share, part), BF16),
         ((n_col, chunk, width), gw_type),
         ((n_col, chunk, width), gw_type),
         ((n_row, chunk, width), gw_type),
@@ -405,7 +426,7 @@
         out_specs=(anywhere, vmem, anywhere, anywhere),
         scratch_shapes=[pltpu.VMEM(shape, kind) for shape, kind in buffers] + [
             pltpu.SMEM((index_rows, slots), jnp.int32),
-            dma((CHUNKS,)), dma(()), dma((6,)), dma((3,)),
+            dma((CHUNKS,)), dma(()), dma((5 + PARTS,)), dma((3,)),
             row_sem, row_sem, chip_sem, chip_sem, chip_sem, chip_sem, chip_sem, chip_sem,
             chip_sem, chip_sem, row_sem, row_sem,
             col_sem, col_sem, row_sem, row_sem, col_sem, col_sem, row_sem, row_sem,

time: 41.1 us -> 39.2 us (0.954)
  Pallas kernels: 39.6 us -> 37.8 us
    pallas_call x1, Pallas kernels: 37.6 us -> 35.8 us  [body(): pl.pallas_call(functools.partial(kernel, n_row, n_col, row_tiles, col_til...]
where the time goes in v5:
time: 39.2 us; the launch traced here: 39.1 us
  Pallas kernels  37.8 us (96%)
  between operations  1.29 us (3%)
    pallas_call x1, Pallas kernels, body(): pl.pallas_call(functools.partial(kernel, n_row, n_col, row_tiles, col_til...  35.8 us
    pallas_call x1, Pallas kernels, body(): pl.pallas_call(finish, out_shape=(jax.ShapeDtypeStruct((share, width), BF...  2 us

profile of v5, /device:TPU:0, one launch (start us, length us, event | category | flops | bytes accessed | tf_op | source)
XLA Modules:
  0.0 39.1 jit_solution(5975609597150451620)
XLA Ops:
  1.3 35.8 %shard_map.111 = (bf16[128,256]{1,0:T(8,128)(2,1)}, bf16[128,256]{1,0:T(8,128)(2,1)}, bf16[8,32,256]{2,1,0:T(8,128)(2,1)}, f32[4,8,256]{2,1,0:T(8,128)}) custom-call(bf16[128,256]{1,0:T(8,128)(2,1)} %feat_ref.1, bf16[256,256]{1,0:T(8,128)(2,1)} %weight_ref.1, f32[1,256]{1,0:T(1,128)} %bitcast.6, bf16[128,256]{1,0:T(8,128)(2,1)} %gout_hbm.1, ...), custom_call_target="tpu_custom_call" | custom-call | flops 536870912 | bytes 4194304 | tf_op jit(solution)/shard_map/pallas_call | solution.py:417
  37.1 2.0 %shard_map.112 = (bf16[128,256]{1,0:T(8,128)(2,1)}, bf16[128,256]{1,0:T(8,128)(2,1)}, f32[256,256]{1,0:T(8,128)}, f32[1,256]{1,0:T(1,128)}) custom-call(bf16[128,256]{1,0:T(8,128)(2,1)} %get-tuple-element.12.part_ref, bf16[128,256]{1,0:T(8,128)(2,1)} %get-tuple-element.13.gmix_ref, bf16[8,32,256]{2,1,0:T(8,128)(2,1)} %get-tuple-element.14.gwp_ref, ...), custom_call_target="tpu_custom_call" | custom-call | tf_op jit(solution)/shard_map/pallas_call | solution.py:441

commit v6 on v5

--- a/solution.py
+++ b/solution.py
@@ -49,6 +49,14 @@
     def lanes(h):
         return slice(h * part, (h + 1) * part)
 
+    row_order, chip_order = list(range(1, n_row)), list(range(1, n_chip))
+    if n_row == 4:
+        turned = 2 * lax.rem(my_r, 2)
+        row_order = [2, 3 - turned, 1 + turned]
+    if n_chip == 4:
+        turned = 2 * lax.rem(chip, 2)
+        chip_order = [3 - turned, 2, 1 + turned]
+
     def row_peer(d):
         return lax.rem(my_r + d, n_row)
 
@@ -98,7 +106,7 @@
         return to_row(feat_ref.at[:, lanes(h)], feat_all.at[h, my_r], f_send, f_recv, d, h)
 
     for h in range(PARTS):
-        for d in range(1, n_row):
+        for d in row_order:
             feat_copy(d, h).start()
 
     tiles = row_tiles * col_tiles
@@ -193,10 +201,11 @@
         for d in range(1, n_row):
             feat_copy(d, h).wait_recv()
         group(n_chip, pair_step)
-        for d in range(n_chip):
-            pair_copy((d + 1) % n_chip, h).start()
+        for d in chip_order:
+            pair_copy(d, h).start()
+        pair_copy(0, h).start()
         group(n_chip, own_step)
-        for d in range(1, n_chip):
+        for d in chip_order:
             pair_copy(d, h).wait_recv()
             part_send[h, d] = (
                 own_sum[h, chip_rows(d), :] + pair_recv[h, d].astype(F32)).astype(BF16)
@@ -242,7 +251,7 @@
         return to_col(rows_of(at, h), rows_of(at, h), h_send, h_recv, d, sibling, h)
 
     for h in range(PARTS):
-        for d in range(1, n_chip):
+        for d in chip_order:
             grad_copy(d, h).start()
         hand_copy(0, h).start()
     out_ref[...] = jnp.where(pre > 0, pre, low - 1.0).astype(BF16)
@@ -276,8 +285,7 @@
         def first_step(start, count):
             back_sum[h, rows_at(start, count), :] = half_product(start, count, core, h)
 
-        def backward_send(i):
-            d = i + 1
+        def backward_send(d):
             back_send[h, d] = backward(row_peer(d), h).astype(BF16)
             back_copy(d, h).start()
 
@@ -287,7 +295,11 @@
         group(n_row, first_step)
         for d in range(n_chip):
             hand_copy(d, h).wait_recv()
-        each(n_row - 1, backward_send)
+        if n_row <= 8:
+            for d in row_order:
+                backward_send(d)
+        else:
+            each(n_row - 1, lambda i: backward_send(i + 1))
         if h == 0:
             gw_sum = gw_send[my_c].astype(F32)
             for d in range(1, n_col):

time: 39.2 us -> 41.1 us (1.048)
  Pallas kernels: 37.8 us -> 39.6 us
    pallas_call x1, Pallas kernels: 35.8 us -> 37.6 us  [body(): pl.pallas_call(functools.partial(kernel, n_row, n_col, row_tiles, col_til...]
where the time goes in v6:
time: 41.1 us; the launch traced here: 40.9 us
  Pallas kernels  39.6 us (96%)
  between operations  1.29 us (3%)
    pallas_call x1, Pallas kernels, body(): pl.pallas_call(functools.partial(kernel, n_row, n_col, row_tiles, col_til...  37.6 us
    pallas_call x1, Pallas kernels, body(): pl.pallas_call(finish, out_shape=(jax.ShapeDtypeStruct((share, width), BF...  2 us

profile of v6, /device:TPU:0, one launch (start us, length us, event | category | flops | bytes accessed | tf_op | source)
XLA Modules:
  0.0 40.9 jit_solution(1626375919359593885)
XLA Ops:
  1.3 37.6 %shard_map.111 = (bf16[128,256]{1,0:T(8,128)(2,1)}, bf16[128,256]{1,0:T(8,128)(2,1)}, bf16[8,32,256]{2,1,0:T(8,128)(2,1)}, f32[4,8,256]{2,1,0:T(8,128)}) custom-call(bf16[128,256]{1,0:T(8,128)(2,1)} %feat_ref.1, bf16[256,256]{1,0:T(8,128)(2,1)} %weight_ref.1, f32[1,256]{1,0:T(1,128)} %bitcast.6, bf16[128,256]{1,0:T(8,128)(2,1)} %gout_hbm.1, ...), custom_call_target="tpu_custom_call" | custom-call | flops 536870912 | bytes 4194304 | tf_op jit(solution)/shard_map/pallas_call | solution.py:429
  38.9 2.0 %shard_map.112 = (bf16[128,256]{1,0:T(8,128)(2,1)}, bf16[128,256]{1,0:T(8,128)(2,1)}, f32[256,256]{1,0:T(8,128)}, f32[1,256]{1,0:T(1,128)}) custom-call(bf16[128,256]{1,0:T(8,128)(2,1)} %get-tuple-element.12.part_ref, bf16[128,256]{1,0:T(8,128)(2,1)} %get-tuple-element.13.gmix_ref, bf16[8,32,256]{2,1,0:T(8,128)(2,1)} %get-tuple-element.14.gwp_ref, ...), custom_call_target="tpu_custom_call" | custom-call | tf_op jit(solution)/shard_map/pallas_call | solution.py:453

commit v7 on v5

--- a/solution.py
+++ b/solution.py
@@ -98,7 +98,7 @@
         return to_row(feat_ref.at[:, lanes(h)], feat_all.at[h, my_r], f_send, f_recv, d, h)
 
     for h in range(PARTS):
-        for d in range(1, n_row):
+        for d in sorted(range(1, n_row), key=lambda d: abs(2 * d - n_row)):
             feat_copy(d, h).start()
 
     tiles = row_tiles * col_tiles

time: 39.2 us -> 41.5 us (1.059)
  Pallas kernels: 37.8 us -> 40 us
    pallas_call x1, Pallas kernels: 35.8 us -> 38 us  [body(): pl.pallas_call(functools.partial(kernel, n_row, n_col, row_tiles, col_til...]
where the time goes in v7:
time: 41.5 us; the launch traced here: 41.3 us
  Pallas kernels  40 us (96%)
  between operations  1.29 us (3%)
    pallas_call x1, Pallas kernels, body(): pl.pallas_call(functools.partial(kernel, n_row, n_col, row_tiles, col_til...  38 us
    pallas_call x1, Pallas kernels, body(): pl.pallas_call(finish, out_shape=(jax.ShapeDtypeStruct((share, width), BF...  2 us

profile of v7, /device:TPU:0, one launch (start us, length us, event | category | flops | bytes accessed | tf_op | source)
XLA Modules:
  0.0 41.3 jit_solution(14269422287169924818)
XLA Ops:
  1.3 38.0 %shard_map.111 = (bf16[128,256]{1,0:T(8,128)(2,1)}, bf16[128,256]{1,0:T(8,128)(2,1)}, bf16[8,32,256]{2,1,0:T(8,128)(2,1)}, f32[4,8,256]{2,1,0:T(8,128)}) custom-call(bf16[128,256]{1,0:T(8,128)(2,1)} %feat_ref.1, bf16[256,256]{1,0:T(8,128)(2,1)} %weight_ref.1, f32[1,256]{1,0:T(1,128)} %bitcast.6, bf16[128,256]{1,0:T(8,128)(2,1)} %gout_hbm.1, ...), custom_call_target="tpu_custom_call" | custom-call | flops 536870912 | bytes 4194304 | tf_op jit(solution)/shard_map/pallas_call | solution.py:417
  39.3 2.0 %shard_map.112 = (bf16[128,256]{1,0:T(8,128)(2,1)}, bf16[128,256]{1,0:T(8,128)(2,1)}, f32[256,256]{1,0:T(8,128)}, f32[1,256]{1,0:T(1,128)}) custom-call(bf16[128,256]{1,0:T(8,128)(2,1)} %get-tuple-element.12.part_ref, bf16[128,256]{1,0:T(8,128)(2,1)} %get-tuple-element.13.gmix_ref, bf16[8,32,256]{2,1,0:T(8,128)(2,1)} %get-tuple-element.14.gwp_ref, ...), custom_call_target="tpu_custom_call" | custom-call | tf_op jit(solution)/shard_map/pallas_call | solution.py:441
